TPU v7x, 128 devices: a whole 4x4x4 slice. The times are simulated.
128 devices in a mesh: section: 4 (over x), dp: 32 (over y, z, core).
Axes of the slice: x: 4, y: 4, z: 4, core: 2. Of those that a mesh axis runs over, the one named last changes fastest.
Arguments:
- patches: bfloat16 [2, 32, 128, 1024], P(None, 'dp'), may hold values from -6 to 6
- segment_ids: int32 [2, 32, 128], P(None, 'dp'), may hold values from 0 to 3, never falling along the last dimension, each value on 1 to 64 neighbouring positions
- weights_qkv: bfloat16 [4, 1024, 3072], P('section'), may hold values from -0.1875 to 0.1875
- weights_out: bfloat16 [4, 1024, 1024], P('section'), may hold values from -0.375 to 0.375
- cotangent: bfloat16 [2, 32, 128, 1024], P(None, 'dp'), may hold values from -6 to 6
Outputs:
- section_outputs: bfloat16 [4, 2, 32, 128, 1024], P('section', None, 'dp')
- section_input_grads: bfloat16 [4, 2, 32, 128, 1024], P('section', None, 'dp')
- grad_qkv: float32 [4, 1024, 3072], P('section', 'dp')
- grad_out: float32 [4, 1024, 1024], P('section', None, 'dp')
Inputs may be any that keep to these rules, and one draw needn't show every extreme that they name: `segment_ids`: within each packed sequence the ids never fall; each image holds 1 to 64 patches, one exactly that many.
All inputs are finite; a program needn't handle non-finite values.
Results may differ from a plain program's by a relative error of at most 0.03.
Values may be sent and summed in bfloat16 or wider, within the bound.
A program may use at most 128 MiB of HBM per device.

v0:
```python
import math

import jax
import jax.numpy as jnp
from jax import lax
from jax.sharding import PartitionSpec as P

HEAD_DIM = 64


epsilon = 1e-06


def passed_along(block, axis, distance):
    devices = range(lax.axis_size(axis))
    route = [(i - distance, i) for i in devices if i - distance in devices]
    return lax.ppermute(block, axis, route)


def layer_norm(values):
    average = jnp.mean(values, axis=-1, keepdims=True)
    centred = values - average
    variance = jnp.mean(centred * centred, axis=-1, keepdims=True)
    return centred * lax.rsqrt(variance + epsilon)


def attend(projected, segments):
    packs, length = segments.shape
    inner = projected.shape[-1] // 3
    queries = layer_norm(projected[..., :inner].reshape(packs, length, -1, HEAD_DIM))
    key_rows = layer_norm(projected[..., inner : 2 * inner].reshape(packs, length, -1, HEAD_DIM))
    value_rows = (
        projected[..., 2 * inner :].astype(jnp.bfloat16).reshape(packs, length, -1, HEAD_DIM)
    )
    scores = jnp.einsum("pshd,pthd->phst", queries, key_rows) / math.sqrt(HEAD_DIM)
    allowed = (segments[:, :, None] == segments[:, None, :])[:, None, :, :]
    weights = jnp.where(allowed, jnp.exp(scores), 0.0)
    probs = (weights / jnp.sum(weights, axis=-1, keepdims=True)).astype(jnp.bfloat16)
    mixed = jnp.einsum("phst,pthd->pshd", probs, value_rows, preferred_element_type=jnp.float32)
    return mixed.reshape(packs, length, inner)


def forward(inputs, segments, w_qkv, w_out):
    packs, length, width = inputs.shape
    widened = inputs.astype(jnp.float32)
    normed = layer_norm(widened).astype(jnp.bfloat16)
    projected = jnp.dot(
        normed.reshape(-1, width), w_qkv, preferred_element_type=jnp.float32
    ).reshape(packs, length, -1)
    mixed = attend(projected, segments).astype(jnp.bfloat16)
    branch = jnp.dot(
        mixed.reshape(-1, mixed.shape[-1]), w_out, preferred_element_type=jnp.float32
    ).reshape(packs, length, width)
    return ((widened + branch).astype(jnp.bfloat16), normed, projected, mixed)


def backward_pieces(inputs, segments, w_qkv, w_out, upstream):
    packs, length, width = inputs.shape
    unused, normed, projected, mixed = forward(inputs, segments, w_qkv, w_out)
    inner = mixed.shape[-1]
    rows = upstream.reshape(-1, width)
    grad_mixed = lax.dot_general(
        rows, w_out, (((1,), (1,)), ((), ())), preferred_element_type=jnp.float32
    )
    grad_mixed = grad_mixed.astype(jnp.bfloat16).reshape(packs, length, inner)
    unused_attend, pull_attend = jax.vjp(lambda values: attend(values, segments), projected)
    grad_projected = pull_attend(grad_mixed.astype(jnp.float32))[0].astype(jnp.bfloat16)
    grad_normed = lax.dot_general(
        grad_projected.reshape(-1, 3 * inner),
        w_qkv,
        (((1,), (1,)), ((), ())),
        preferred_element_type=jnp.float32,
    )
    unused_norm, pull_norm = jax.vjp(layer_norm, inputs.astype(jnp.float32))
    grad_inputs = (
        upstream.astype(jnp.float32) + pull_norm(grad_normed.reshape(packs, length, width))[0]
    )
    return (grad_inputs.astype(jnp.bfloat16), normed, grad_projected, mixed)


def weight_terms(normed, grad_projected, mixed, upstream):
    width = normed.shape[-1]
    inner = mixed.shape[-1]
    part_qkv = lax.dot_general(
        normed.reshape(-1, width),
        grad_projected.reshape(-1, 3 * inner),
        (((0,), (0,)), ((), ())),
        preferred_element_type=jnp.float32,
    )
    part_out = lax.dot_general(
        mixed.reshape(-1, inner),
        upstream.reshape(-1, width),
        (((0,), (0,)), ((), ())),
        preferred_element_type=jnp.float32,
    )
    return (part_qkv, part_out)


def pick(stack, position):
    return lax.dynamic_index_in_dim(stack, position, 0, keepdims=False)


def place(stack, value, position, active):
    updated = lax.dynamic_update_index_in_dim(stack, value, position, 0)
    return jnp.where(active, updated, stack)


def on_device(patches, segment_ids, weights_qkv, weights_out, cotangent):
    section_count = lax.axis_size("section")
    section_index = lax.axis_index("section")
    micro_count = patches.shape[0]
    w_qkv = weights_qkv[0]
    w_out = weights_out[0]
    inner = w_out.shape[0]
    blank = jnp.zeros(patches.shape[1:], jnp.bfloat16)
    stash = jnp.zeros_like(patches)
    produced = jnp.zeros_like(patches)
    moments = micro_count + section_count - 1
    received = blank
    for moment in range(moments):
        offset = moment - section_index
        active = (offset >= 0) & (offset < micro_count)
        micro_slot = jnp.clip(offset, 0, micro_count - 1)
        section_entry = jnp.where(
            section_index == 0, patches[min(moment, micro_count - 1)], received
        )
        segments = pick(segment_ids, micro_slot)
        section_result = lax.cond(
            active, lambda: forward(section_entry, segments, w_qkv, w_out)[0], lambda: blank
        )
        stash = place(stash, section_entry, micro_slot, active)
        produced = place(produced, section_result, micro_slot, active)
        if moment < moments - 1:
            received = passed_along(section_result, "section", 1)
    grad_stash = jnp.zeros_like(patches)
    packs_here = patches.shape[1]
    length = patches.shape[2]
    normed_stash = jnp.zeros_like(patches)
    projgrad_stash = jnp.zeros((micro_count, packs_here, length, 3 * inner), jnp.bfloat16)
    mixed_stash = jnp.zeros((micro_count, packs_here, length, inner), jnp.bfloat16)
    upstream_stash = jnp.zeros_like(patches)
    received = blank
    for moment in range(moments):
        offset = moment - (section_count - 1 - section_index)
        active = (offset >= 0) & (offset < micro_count)
        micro_slot = jnp.clip(offset, 0, micro_count - 1)
        incoming = jnp.where(
            section_index == section_count - 1, pick(cotangent, micro_slot), received
        )
        segments = pick(segment_ids, micro_slot)
        section_entry = pick(stash, micro_slot)

        def run_layer():
            return backward_pieces(section_entry, segments, w_qkv, w_out, incoming)

        def skip_layer():
            return (
                blank,
                blank,
                jnp.zeros((packs_here, length, 3 * inner), jnp.bfloat16),
                jnp.zeros((packs_here, length, inner), jnp.bfloat16),
            )

        grad_inputs, normed, grad_projected, mixed = lax.cond(active, run_layer, skip_layer)
        normed_stash = place(normed_stash, normed, micro_slot, active)
        projgrad_stash = place(projgrad_stash, grad_projected, micro_slot, active)
        mixed_stash = place(mixed_stash, mixed, micro_slot, active)
        upstream_stash = place(upstream_stash, incoming, micro_slot, active)
        grad_stash = place(grad_stash, grad_inputs, micro_slot, active)
        if moment < moments - 1:
            received = passed_along(grad_inputs, "section", -1)
    whole_qkv, whole_out = weight_terms(normed_stash, projgrad_stash, mixed_stash, upstream_stash)
    total_qkv, total_out = (
        lax.psum_scatter(
            whole_qkv.astype(jnp.bfloat16), "dp", scatter_dimension=0, tiled=True
        ).astype(jnp.float32),
        lax.psum_scatter(
            whole_out.astype(jnp.bfloat16), "dp", scatter_dimension=1, tiled=True
        ).astype(jnp.float32),
    )
    return (produced[None], grad_stash[None], total_qkv[None], total_out[None])


def solution(mesh):
    return jax.shard_map(
        on_device,
        mesh=mesh,
        in_specs=(
            P(None, "dp", None, None),
            P(None, "dp", None),
            P("section", None, None),
            P("section", None, None),
            P(None, "dp", None, None),
        ),
        out_specs=(
            P("section", None, "dp", None, None),
            P("section", None, "dp", None, None),
            P("section", "dp", None),
            P("section", None, "dp"),
        ),
        check_vma=False,
    )
```

profile of v0, /device:TPU:0, one launch (start us, length us, event | category | flops | bytes accessed | tf_op | source)
XLA Modules:
  0.0 486.1 jit_solution(15448698014493476725)
XLA Ops:
  8.4 15.1 %conditional.10 = (bf16[1,128,1024]{2,1,0:T(8,128)(2,1)}, bf16[1,1,128,1024]{3,2,1,0:T(8,128)(2,1)S(1)}) conditional(s32[]{:T(128)} %convert_element_type.893, () %tuple.172, (bf16[1,1,128,1024]{3,2,1,0:T(8,128)(2,1)S(1)}, pred[1,128,1024]{2,1,0:T(8,128)(4,1)S(1)}, bf16[1,128,1024]{2,1,0:T(8,128)(2,1)S(1)}, bf16[1024,3072]{1,0:T(8,128)(2,1)}, ...), branch_computations={%region_0.1_spmd, %region_1.9_spmd} | conditional | flops 1145460992 | bytes 33347668 | solution.py:128
  9.0 3.8 convolution_bitcast_fusion
  17.7 2.7 convolution_convert_fusion
  20.4 2.1 fusion.3
  24.8 5.4 %collective-permute-done = bf16[1,128,1024]{2,1,0:T(8,128)(2,1)S(1)} collective-permute-done((bf16[1,128,1024]{2,1,0:T(8,128)(2,1)}, bf16[1,128,1024]{2,1,0:T(8,128)(2,1)S(1)}, u32[]{:S(2)}, u32[]{:S(2)}) %collective-permute-start) | collective-permute-done | bytes 262176 | tf_op jit(solution)/shard_map/ppermute | solution.py:17
  31.3 15.0 %conditional.11 = (bf16[1,128,1024]{2,1,0:T(8,128)(2,1)}, bf16[1,1,128,1024]{3,2,1,0:T(8,128)(2,1)S(1)}) conditional(s32[]{:T(128)} %convert_element_type.894, () %tuple.174, (bf16[1,128,1024]{2,1,0:T(8,128)(2,1)S(1)}, bf16[1024,3072]{1,0:T(8,128)(2,1)}, s32[2,1,128]{2,1,0:T(1,128)S(1)}, s32[]{:T(128)}, bf16[1024,1024]{1,0:T(8,128)(2,1)}) %tuple.322), branch_computations={%region_9.10_spmd, %region_10.18_spmd} | conditional | flops 1145329920 | bytes 32692308 | solution.py:128
  31.8 3.8 convolution_bitcast_fusion.2
  40.5 2.7 convolution_convert_fusion.1
  43.2 2.1 fusion.25
  46.3 4.3 collective-permute-start.1
  50.6 4.4 collective-permute-done.1
  56.9 18.5 %collective-permute-start.2 = (bf16[1,128,1024]{2,1,0:T(8,128)(2,1)}, bf16[1,128,1024]{2,1,0:T(8,128)(2,1)S(1)}, u32[]{:S(2)}, u32[]{:S(2)}) collective-permute-start(bf16[1,128,1024]{2,1,0:T(8,128)(2,1)} %get-tuple-element.506), channel_id=1, source_target_pairs={{0,32},{32,64},{64,96},{1,33},{33,65},{65,97},{2,34},{34,66},{66,9... | collective-permute-start | bytes 786440 | tf_op jit(solution)/shard_map/ppermute | solution.py:17
  75.4 4.2 collective-permute-done.2
  82.4 4.4 collective-permute-start.3
  88.0 3.0 collective-permute-done.3
  92.2 3.2 conditional.15
  97.6 18.8 %collective-permute-done.4 = bf16[1,128,1024]{2,1,0:T(8,128)(2,1)S(1)} collective-permute-done((bf16[1,128,1024]{2,1,0:T(8,128)(2,1)}, bf16[1,128,1024]{2,1,0:T(8,128)(2,1)S(1)}, u32[]{:S(2)}, u32[]{:S(2)}) %collective-permute-start.4) | collective-permute-done | bytes 262176 | tf_op jit(solution)/shard_map/ppermute | solution.py:17
  117.4 3.3 conditional.16
  122.3 7.3 %collective-permute-done.5 = bf16[1,128,1024]{2,1,0:T(8,128)(2,1)S(1)} collective-permute-done((bf16[1,128,1024]{2,1,0:T(8,128)(2,1)}, bf16[1,128,1024]{2,1,0:T(8,128)(2,1)S(1)}, u32[]{:S(2)}, u32[]{:S(2)}) %collective-permute-start.5) | collective-permute-done | bytes 262176 | tf_op jit(solution)/shard_map/ppermute | solution.py:17
  130.6 2.7 conditional.17
  134.7 1.7 select_dynamic-update-slice_fusion.7
  136.4 1.7 select_dynamic-update-slice_fusion.11
  138.2 90.0 %collective-permute-done.6 = bf16[1,128,1024]{2,1,0:T(8,128)(2,1)S(1)} collective-permute-done((bf16[1,128,1024]{2,1,0:T(8,128)(2,1)}, bf16[1,128,1024]{2,1,0:T(8,128)(2,1)S(1)}, u32[]{:S(2)}, u32[]{:S(2)}) %collective-permute-start.6) | collective-permute-done | bytes 262176 | tf_op jit(solution)/shard_map/ppermute | solution.py:17
  229.1 32.1 %conditional.18 = (bf16[1,128,1024]{2,1,0:T(8,128)(2,1)}, bf16[1,1,128,1024]{3,2,1,0:T(8,128)(2,1)}, bf16[1,1,128,1024]{3,2,1,0:T(8,128)(2,1)}, bf16[1,1,128,307...) conditional(s32[]{:T(128)} %convert_element_type.901, () %tuple.188, (bf16[1,128,1024]{2,1,0:T(8,128)(2,1)S(1)}, ...), branch_computations={%region_93.94_spmd, %region_94.109_spmd} | conditional | flops 2100607872 | bytes 88963960 | solution.py:164
  232.4 3.8 convolution_bitcast_fusion.19
  239.3 2.0 copy.180
  247.8 1.8 copy.241
  249.7 2.1 multiply_reduce_fusion.22
  251.8 1.8 multiply_reduce_fusion.23
  255.0 2.3 fusion.266
  262.6 2.0 select_dynamic-update-slice_fusion.6
  264.7 1.9 select_dynamic-update-slice_fusion.5
  266.5 1.9 copy.344
  270.7 30.3 %conditional.19 = (bf16[1,1,128,1024]{3,2,1,0:T(8,128)(2,1)}, bf16[1,1,128,1024]{3,2,1,0:T(8,128)(2,1)}, bf16[1,1,128,3072]{2,3,1,0:T(8,128)(2,1)}, bf16[1,1,128,1024]{3,2,1,0:T(8,128)(2,1)}) conditional(s32[]{:T(128)} %convert_element_type.902, () %tuple.190, (bf16[1,128,1024]{2,1,0:T(8,128)(2,1)S(1)}, bf16[1024,1024]{1,0:T(8,128)(2,1)S(1)}, ...), branch_computations={%region_109.110_spmd, %region_110.125_spmd} | conditional | flops 2100607872 | bytes 88439664 | solution.py:164
  274.1 3.8 convolution_bitcast_fusion.22
  280.9 2.0 copy.191
  289.4 1.8 copy.243
  291.2 2.1 multiply_reduce_fusion.26
  293.4 1.8 multiply_reduce_fusion.27
  296.5 2.3 fusion.313
  301.1 1.8 bitcast_dynamic-update-slice_fusion.3
  302.9 3.3 bitcast_convert_fusion.1
  306.5 2.2 select_dynamic-update-slice_fusion.2
  308.8 2.3 select_dynamic-update-slice_fusion.1
  316.5 4.5 bitcast_convert_fusion
  327.2 60.4 %reduce-scatter.5.cloned.1.call-done = bf16[1024,32]{0,1:T(8,128)(2,1)} async-done(((bf16[1024,1024]{0,1:T(8,128)(2,1)}), bf16[1024,32]{0,1:T(8,128)(2,1)}) %reduce-scatter.5.cloned.1.call-update) | async-done | bytes 65552 | tf_op jit(solution)/shard_map/reduce_scatter | solution.py:177
  389.2 87.9 %reduce-scatter.3.cloned.1.call-done = bf16[32,3072]{1,0:T(8,128)(2,1)} async-done(((bf16[1024,3072]{1,0:T(8,128)(2,1)}), bf16[32,3072]{1,0:T(8,128)(2,1)}) %reduce-scatter.3.cloned.1.call-update) | async-done | bytes 196624 | tf_op jit(solution)/shard_map/reduce_scatter | solution.py:174
  477.1 1.7 bitcast_convert_fusion.2
  (317 shorter events, 93.8 us)
Async XLA Ops:
  7.2 380.5 %reduce-scatter.5.cloned.1.call-start = ((), (), s32[]{:S(2)}) async-start(), calls=%async_computation.3 | async-start | bytes 2162688 | tf_op jit(solution)/shard_map/reduce_scatter | solution.py:177
  17.7 2.7 copy-start.1
  23.5 7.8 %copy-start.60 = (bf16[1,1,128,1024]{3,2,1,0:T(8,128)(2,1)}, bf16[1,1,128,1024]{3,2,1,0:T(8,128)(2,1)S(1)}, u32[]{:S(2)}) copy-start(bf16[1,1,128,1024]{3,2,1,0:T(8,128)(2,1)S(1)} %get-tuple-element.501) | copy-start | bytes 786436
  23.5 6.7 %collective-permute-start = (bf16[1,128,1024]{2,1,0:T(8,128)(2,1)}, bf16[1,128,1024]{2,1,0:T(8,128)(2,1)S(1)}, u32[]{:S(2)}, u32[]{:S(2)}) collective-permute-start(bf16[1,128,1024]{2,1,0:T(8,128)(2,1)} %get-tuple-element.502), channel_id=1, source_target_pairs={{0,32},{32,64},{64,96},{1,33},{33,65},{65,97},{2,34},{34,66},{66,9... | collective-permute-start | bytes 786440 | tf_op jit(solution)/shard_map/ppermute | solution.py:17
  40.5 2.7 copy-start.2
  46.3 9.9 %copy-start.62 = (bf16[1,1,128,1024]{3,2,1,0:T(8,128)(2,1)}, bf16[1,1,128,1024]{3,2,1,0:T(8,128)(2,1)S(1)}, u32[]{:S(2)}) copy-start(bf16[1,1,128,1024]{3,2,1,0:T(8,128)(2,1)S(1)} %get-tuple-element.503) | copy-start | bytes 786436
  46.3 8.7 %collective-permute-start.1 = (bf16[1,128,1024]{2,1,0:T(8,128)(2,1)}, bf16[1,128,1024]{2,1,0:T(8,128)(2,1)S(1)}, u32[]{:S(2)}, u32[]{:S(2)}) collective-permute-start(bf16[1,128,1024]{2,1,0:T(8,128)(2,1)} %get-tuple-element.504), channel_id=1, source_target_pairs={{0,32},{32,64},{64,96},{1,33},{33,65},{65,97},{2,34},{34,66},{66,9... | collective-permute-start | bytes 786440 | tf_op jit(solution)/shard_map/ppermute | solution.py:17
  56.9 23.8 %copy-start.64 = (bf16[1,1,128,1024]{3,2,1,0:T(8,128)(2,1)}, bf16[1,1,128,1024]{3,2,1,0:T(8,128)(2,1)S(1)}, u32[]{:S(2)}) copy-start(bf16[1,1,128,1024]{3,2,1,0:T(8,128)(2,1)S(1)} %get-tuple-element.505) | copy-start | bytes 786436
  56.9 22.7 %collective-permute-start.2 = (bf16[1,128,1024]{2,1,0:T(8,128)(2,1)}, bf16[1,128,1024]{2,1,0:T(8,128)(2,1)S(1)}, u32[]{:S(2)}, u32[]{:S(2)}) collective-permute-start(bf16[1,128,1024]{2,1,0:T(8,128)(2,1)} %get-tuple-element.506), channel_id=1, source_target_pairs={{0,32},{32,64},{64,96},{1,33},{33,65},{65,97},{2,34},{34,66},{66,9... | collective-permute-start | bytes 786440 | tf_op jit(solution)/shard_map/ppermute | solution.py:17
  82.4 9.8 %copy-start = (bf16[1,1024,1024]{2,1,0:T(8,128)(2,1)S(1)}, bf16[1,1024,1024]{2,1,0:T(8,128)(2,1)}, u32[]{:S(2)}) copy-start(bf16[1,1024,1024]{2,1,0:T(8,128)(2,1)} %param.28) | copy-start | bytes 6291460
  82.4 8.6 %collective-permute-start.3 = (bf16[1,128,1024]{2,1,0:T(8,128)(2,1)}, bf16[1,128,1024]{2,1,0:T(8,128)(2,1)S(1)}, u32[]{:S(2)}, u32[]{:S(2)}) collective-permute-start(bf16[1,128,1024]{2,1,0:T(8,128)(2,1)} %get-tuple-element.508), channel_id=1, source_target_pairs={{0,32},{32,64},{64,96},{1,33},{33,65},{65,97},{2,34},{34,66},{66,9... | collective-permute-start | bytes 786440 | tf_op jit(solution)/shard_map/ppermute | solution.py:17
  88.0 4.2 copy-start.20
  95.4 1.7 copy-start.55
  95.4 21.0 %collective-permute-start.4 = (bf16[1,128,1024]{2,1,0:T(8,128)(2,1)}, bf16[1,128,1024]{2,1,0:T(8,128)(2,1)S(1)}, u32[]{:S(2)}, u32[]{:S(2)}) collective-permute-start(bf16[1,128,1024]{2,1,0:T(8,128)(2,1)} %get-tuple-element.510), channel_id=1, source_target_pairs={{32,0},{64,32},{96,64},{33,1},{65,33},{97,65},{34,2},{66,34},{98,6... | collective-permute-start | bytes 786440 | tf_op jit(solution)/shard_map/ppermute | solution.py:17
  97.1 19.3 %copy-start.21 = (bf16[2,1,128,1024]{3,2,1,0:T(8,128)(2,1)S(1)}, bf16[2,1,128,1024]{3,2,1,0:T(8,128)(2,1)}, u32[]{:S(2)}) copy-start(bf16[2,1,128,1024]{3,2,1,0:T(8,128)(2,1)} %copy-done.20) | copy-start | bytes 1572868
  97.1 19.3 %copy-start.30 = (bf16[2,1,128,1024]{3,2,1,0:T(8,128)(2,1)S(1)}, bf16[2,1,128,1024]{3,2,1,0:T(8,128)(2,1)}, u32[]{:S(2)}) copy-start(bf16[2,1,128,1024]{3,2,1,0:T(8,128)(2,1)} %param.29) | copy-start | bytes 1572868
  97.4 19.2 %copy-start.107 = (s32[2,1,128]{2,1,0:T(1,128)S(1)}, s32[2,1,128]{2,1,0:T(1,128)}, u32[]{:S(2)}) copy-start(s32[2,1,128]{2,1,0:T(1,128)} %param.26) | copy-start | bytes 3076
  97.6 19.0 %copy-start.5 = (bf16[2,1,128,3072]{2,3,1,0:T(8,128)(2,1)}, bf16[2,1,128,3072]{2,3,1,0:T(8,128)(2,1)S(1)}, u32[]{:S(2)}) copy-start(bf16[2,1,128,3072]{2,3,1,0:T(8,128)(2,1)S(1)} %select_dynamic-update-slice_fusion.3) | copy-start | bytes 4718596
  120.6 9.0 %copy-start.23 = (bf16[2,1,128,1024]{3,2,1,0:T(8,128)(2,1)S(1)}, bf16[2,1,128,1024]{3,2,1,0:T(8,128)(2,1)}, u32[]{:S(2)}) copy-start(bf16[2,1,128,1024]{3,2,1,0:T(8,128)(2,1)} %copy-done.22) | copy-start | bytes 1572868
  120.6 9.0 %copy-start.31 = (bf16[2,1,128,1024]{3,2,1,0:T(8,128)(2,1)S(1)}, bf16[2,1,128,1024]{3,2,1,0:T(8,128)(2,1)}, u32[]{:S(2)}) copy-start(bf16[2,1,128,1024]{3,2,1,0:T(8,128)(2,1)} %param.29) | copy-start | bytes 1572868
  120.6 9.0 %collective-permute-start.5 = (bf16[1,128,1024]{2,1,0:T(8,128)(2,1)}, bf16[1,128,1024]{2,1,0:T(8,128)(2,1)S(1)}, u32[]{:S(2)}, u32[]{:S(2)}) collective-permute-start(bf16[1,128,1024]{2,1,0:T(8,128)(2,1)} %get-tuple-element.512), channel_id=1, source_target_pairs={{32,0},{64,32},{96,64},{33,1},{65,33},{97,65},{34,2},{66,34},{98,6... | collective-permute-start | bytes 786440 | tf_op jit(solution)/shard_map/ppermute | solution.py:17
  122.2 7.6 %copy-start.17 = (bf16[2,1,128,1024]{3,2,1,0:T(8,128)(2,1)}, bf16[2,1,128,1024]{3,2,1,0:T(8,128)(2,1)S(1)}, u32[]{:S(2)}) copy-start(bf16[2,1,128,1024]{3,2,1,0:T(8,128)(2,1)S(1)} %select_dynamic-update-slice_fusion.8) | copy-start | bytes 1572868
  122.3 7.4 %copy-start.18 = (bf16[2,1,128,1024]{3,2,1,0:T(8,128)(2,1)}, bf16[2,1,128,1024]{3,2,1,0:T(8,128)(2,1)S(1)}, u32[]{:S(2)}) copy-start(bf16[2,1,128,1024]{3,2,1,0:T(8,128)(2,1)S(1)} %select_dynamic-update-slice_fusion.12) | copy-start | bytes 1572868
  133.2 95.1 %copy-start.58 = (bf16[1,1,128,1024]{3,2,1,0:T(8,128)(2,1)}, bf16[1,1,128,1024]{3,2,1,0:T(8,128)(2,1)S(1)}, u32[]{:S(2)}) copy-start(bf16[1,1,128,1024]{3,2,1,0:T(8,128)(2,1)S(1)} %get-tuple-element.513) | copy-start | bytes 786436
  133.2 95.1 %copy-start.77 = (bf16[1,1,128,1024]{3,2,1,0:T(8,128)(2,1)}, bf16[1,1,128,1024]{3,2,1,0:T(8,128)(2,1)S(1)}, u32[]{:S(2)}) copy-start(bf16[1,1,128,1024]{3,2,1,0:T(8,128)(2,1)S(1)} %get-tuple-element.520) | copy-start | bytes 786436
  133.2 94.9 %copy-start.25 = (bf16[2,1,128,1024]{3,2,1,0:T(8,128)(2,1)S(1)}, bf16[2,1,128,1024]{3,2,1,0:T(8,128)(2,1)}, u32[]{:S(2)}) copy-start(bf16[2,1,128,1024]{3,2,1,0:T(8,128)(2,1)} %copy-done.24) | copy-start | bytes 1572868
  133.2 94.9 %copy-start.32 = (bf16[2,1,128,1024]{3,2,1,0:T(8,128)(2,1)S(1)}, bf16[2,1,128,1024]{3,2,1,0:T(8,128)(2,1)}, u32[]{:S(2)}) copy-start(bf16[2,1,128,1024]{3,2,1,0:T(8,128)(2,1)} %param.29) | copy-start | bytes 1572868
  133.3 94.9 %collective-permute-start.6 = (bf16[1,128,1024]{2,1,0:T(8,128)(2,1)}, bf16[1,128,1024]{2,1,0:T(8,128)(2,1)S(1)}, u32[]{:S(2)}, u32[]{:S(2)}) collective-permute-start(bf16[1,128,1024]{2,1,0:T(8,128)(2,1)} %get-tuple-element.514), channel_id=1, source_target_pairs={{32,0},{64,32},{96,64},{33,1},{65,33},{97,65},{34,2},{66,34},{98,6... | collective-permute-start | bytes 786440 | tf_op jit(solution)/shard_map/ppermute | solution.py:17
  239.3 2.0 copy-start.13
  242.7 1.7 copy-start.69
  242.7 1.7 copy-start.74
  249.6 2.1 copy-start.14
  249.6 2.1 copy-start.52
  249.7 4.7 slice-start.6
  251.8 2.6 slice-start.7
  261.2 3.5 copy-start.27
  261.2 8.6 %collective-permute-start.7 = (bf16[1,128,1024]{2,1,0:T(8,128)(2,1)}, bf16[1,128,1024]{2,1,0:T(8,128)(2,1)S(1)}, u32[]{:S(2)}, u32[]{:S(2)}) collective-permute-start(bf16[1,128,1024]{2,1,0:T(8,128)(2,1)} %get-tuple-element.516), channel_id=1, source_target_pairs={{32,0},{64,32},{96,64},{33,1},{65,33},{97,65},{34,2},{66,34},{98,6... | collective-permute-start | bytes 786440 | tf_op jit(solution)/shard_map/ppermute | solution.py:17
  264.6 5.1 %copy-start.33 = (bf16[2,1,128,1024]{3,2,1,0:T(8,128)(2,1)S(1)}, bf16[2,1,128,1024]{3,2,1,0:T(8,128)(2,1)}, u32[]{:S(2)}) copy-start(bf16[2,1,128,1024]{3,2,1,0:T(8,128)(2,1)} %param.29) | copy-start | bytes 1572868
  280.9 2.0 copy-start.15
  284.3 1.7 copy-start.70
  284.4 1.7 copy-start.75
  291.2 2.1 copy-start.16
  291.2 2.1 copy-start.54
  291.2 4.7 slice-start.8
  293.3 2.6 slice-start.9
  306.2 170.9 %reduce-scatter.3.cloned.1.call-start = ((), (), s32[]{:S(2)}) async-start(), calls=%async_computation.2 | async-start | bytes 6488064 | tf_op jit(solution)/shard_map/reduce_scatter | solution.py:174
  308.8 2.3 copy-start.19
  327.2 151.5 %copy-start.83 = (bf16[1,2,1,128,1024]{4,3,2,1,0:T(8,128)(2,1)}, bf16[1,2,1,128,1024]{4,3,2,1,0:T(8,128)(2,1)S(1)}, u32[]{:S(2)}) copy-start(bf16[1,2,1,128,1024]{4,3,2,1,0:T(8,128)(2,1)S(1)} %bitcast_dynamic-update-slice_fusion.5) | copy-start | bytes 1572868
  (22 other events, 25.4 us)
Sparse Core Ops, SparseCore 0:
  306.3 81.3 reduce-scatter.4
  391.4 85.6 reduce-scatter.2
where the time goes:
time: 495 us; the launch traced here: 486 us
  waiting for transfers between devices  283 us (57%)
  matrix products  59.3 us (12%)
  local copies, waits for them, and re-layouts  48.9 us (10%)
  other arithmetic  43.3 us (9%)
  starting transfers between devices  34.8 us (7%)
  between operations  15.3 us (3%)
    ppermute x8, waiting for transfers between devices, passed_along(): return lax.ppermute(block, axis, route)  134 us
    reduce_scatter x1, waiting for transfers between devices, on_device(): lax.psum_scatter(whole_qkv.astype(jnp.bfloat16), 'dp', scatter_dimension=...  87.9 us
    reduce_scatter x1, waiting for transfers between devices, on_device(): lax.psum_scatter(whole_out.astype(jnp.bfloat16), 'dp', scatter_dimension=...  60.4 us
    ppermute x8, starting transfers between devices, passed_along(): return lax.ppermute(block, axis, route)  34.4 us
    select_n x34, other arithmetic, place(): return jnp.where(active, updated, stack)  29.4 us
    dot_general x4, matrix products, forward(): jnp.dot(normed.reshape(-1, width), w_qkv, preferred_element_type=jnp.floa...  15.3 us
    dot_general x8, matrix products, attend(): jnp.einsum('pshd,pthd->phst', queries, key_rows) / math.sqrt(HEAD_DIM)  13.5 us
    dot_general x8, matrix products, attend(): jnp.einsum('phst,pthd->pshd', probs, value_rows, preferred_element_type=j...  12.2 us
  transfers between devices with their start and end apart: 10, of which 10 were waited for; matrix products, arithmetic and copies ran while one was open for 7% of the time, Pallas kernels for 0%

commit v1 on v0

v1 whole, which is shorter than its diff:
```python
import functools

import jax
import jax.numpy as jnp
from jax import lax
from jax.experimental import pallas as pl
from jax.experimental.pallas import tpu as pltpu
from jax.sharding import PartitionSpec as P

BF16 = jnp.bfloat16
F32 = jnp.float32
EPSILON = 1e-6
MESH = pl.DeviceIdType.MESH


def dg(a,b,ca=1,cb=0): return lax.dot_general(a,b,(((ca,),(cb,)),((),())),preferred_element_type=F32)

def block_diagonal(pair):
    blank = jnp.zeros((64, pair.shape[1]), pair.dtype)
    top = jnp.concatenate([pair[:64], blank], axis=1)
    bottom = jnp.concatenate([blank, pair[64:]], axis=1)
    return jnp.concatenate([top, bottom], axis=0)

def head_norm(rows):
    grouped = rows.reshape(2, 64, rows.shape[1])
    centred = grouped - jnp.mean(grouped, axis=1, keepdims=True)
    inverse = lax.rsqrt(jnp.mean(centred * centred, axis=1, keepdims=True) + EPSILON)
    return (centred * inverse).reshape(rows.shape), inverse[:, 0, :]

def head_norm_pull(grad, normed, inverse):
    tokens = grad.shape[1]
    g = grad.reshape(2, 64, tokens)
    n = normed.reshape(2, 64, tokens)
    first = jnp.mean(g, axis=1, keepdims=True)
    second = jnp.mean(g * n, axis=1, keepdims=True)
    return ((g - first - n * second) * inverse[:, None, :]).reshape(grad.shape)

def forward_step(m, r):
    x = r["xin"][m].astype(F32)
    centred = x - jnp.mean(x, axis=-1, keepdims=True)
    inverse = lax.rsqrt(jnp.mean(centred * centred, axis=-1, keepdims=True) + EPSILON)
    r["xinv"][m] = jnp.broadcast_to(inverse, (128, 128))
    r["normed"][m] = (centred * inverse).astype(BF16)
    queries_in = jnp.broadcast_to(r["segments"][m].astype(F32), (128, 128))
    allowed = queries_in == queries_in.T
    allowed = jnp.concatenate([allowed, allowed], axis=1)
    for quad in range(4):
        normed = r["normed"][m]
        q4 = dg(normed, r["wqkv"][:, 256*quad:256*quad+256])
        k4 = dg(normed, r["wqkv"][:, 1024+256*quad:1024+256*quad+256])
        v4 = dg(normed, r["wqkv"][:, 2048+256*quad:2048+256*quad+256]).astype(BF16)
        for half in range(2):
            pair = 2*quad+half
            c = slice(128*half, 128*half+128)
            q, qi = head_norm(q4[:, c].T)
            k, ki = head_norm(k4[:, c].T)
            qs = (q * 0.125).astype(BF16)
            kt = k.astype(BF16)
            v = v4[:, c]
            r["qs"][m, pair] = qs
            r["kt"][m, pair] = kt
            r["v"][m, pair] = v
            r["qi"][m, pair] = qi
            r["ki"][m, pair] = ki
            scores = dg(kt.T, block_diagonal(qs))
            w = jnp.where(allowed, jnp.exp(scores), 0.0)
            p = (w * (1.0 / jnp.sum(w, axis=0, keepdims=True))).astype(BF16)
            r["probs"][m, pair] = p
            vt = v.T
            o = jnp.concatenate([dg(vt[:64], p[:, :128]), dg(vt[64:], p[:, 128:])], axis=0).astype(BF16)
            r["mixed"][m, :, 128*pair:128*pair+128] = o.T
    mixed = r["mixed"][m]
    for j in range(4):
        c = slice(256*j, 256*j+256)
        branch = dg(mixed, r["wout"][:, c])
        r["xout"][m, :, c] = (r["xin"][m, :, c].astype(F32) + branch).astype(BF16)

def backward_step(m, r):
    g = r["gin"][m]
    for quad in range(4):
        go4 = dg(g, r["wout_t"][:, 256*quad:256*quad+256]).astype(BF16)
        for half in range(2):
            pair = 2*quad+half
            go = go4[:, 128*half:128*half+128]
            got = go.T
            p = r["probs"][m, pair]
            dp = dg(r["v"][m, pair], block_diagonal(got))
            pd = p.astype(F32) * dp
            ds = (pd - p.astype(F32) * jnp.sum(pd, axis=0, keepdims=True)).astype(BF16)
            kt = r["kt"][m, pair]; qs = r["qs"][m, pair]
            gq = jnp.concatenate([dg(kt[:64], ds[:, :128]), dg(kt[64:], ds[:, 128:])], axis=0)
            gk = jnp.concatenate([dg(qs[:64], ds[:, :128], 1, 1), dg(qs[64:], ds[:, 128:], 1, 1)], axis=0)
            gv = jnp.concatenate([dg(got[:64], p[:, :128], 1, 1), dg(got[64:], p[:, 128:], 1, 1)], axis=0).astype(BF16).T
            gq = head_norm_pull(gq * 0.125, qs.astype(F32) * 8.0, r["qi"][m, pair])
            gk = head_norm_pull(gk, kt.astype(F32), r["ki"][m, pair])
            r["gproj"][m, :, 128*pair:128*pair+128] = gq.astype(BF16).T
            r["gproj"][m, :, 1024+128*pair:1024+128*pair+128] = gk.astype(BF16).T
            r["gproj"][m, :, 2048+128*pair:2048+128*pair+128] = gv
    gproj = r["gproj"][m]
    for j in range(4):
        r["gn"][:, 256*j:256*j+256] = dg(gproj, r["wqkv_t"][:, 256*j:256*j+256])
    gn = r["gn"][...]
    n = r["normed"][m].astype(F32)
    first = jnp.mean(gn, axis=-1, keepdims=True)
    second = jnp.mean(gn * n, axis=-1, keepdims=True)
    dx = (gn - first - n * second) * r["xinv"][m][:, :1]
    r["gout"][m] = (r["gin"][m].astype(F32) + dx).astype(BF16)

def transpose_weights(r):
    for j in range(8):
        r["wqkv_t"][:, 128*j:128*j+128] = r["wqkv"][128*j:128*j+128, :].T
        r["wout_t"][:, 128*j:128*j+128] = r["wout"][128*j:128*j+128, :].T


def relay_kernel(names, *refs):
    r = dict(zip(names, refs))
    section = lax.axis_index("section")
    last = lax.axis_size("section") - 1
    after = lax.rem(section + 1, last + 1)
    before = lax.rem(section + last, last + 1)
    is_first = section == 0
    is_last = section == last

    loads = [
        pltpu.make_async_copy(r["w_qkv_hbm"].at[0], r["wqkv"], r["load"].at[0]),
        pltpu.make_async_copy(r["w_out_hbm"].at[0], r["wout"], r["load"].at[1]),
    ]

    def entry(m):
        return pltpu.make_async_copy(r["patches"].at[m, 0], r["xin"].at[m], r["load"].at[2 + m])

    def end_gradient(m):
        return pltpu.make_async_copy(r["cotangent"].at[m, 0], r["gin"].at[m], r["load"].at[4 + m])

    def pass_on(m):
        return pltpu.make_async_remote_copy(
            src_ref=r["xout"].at[m], dst_ref=r["xin"].at[m],
            send_sem=r["x_send"].at[m], recv_sem=r["x_recv"].at[m],
            device_id={"section": after}, device_id_type=MESH,
        )

    def pass_back(m):
        return pltpu.make_async_remote_copy(
            src_ref=r["gout"].at[m], dst_ref=r["gin"].at[m],
            send_sem=r["g_send"].at[m], recv_sem=r["g_recv"].at[m],
            device_id={"section": before}, device_id_type=MESH,
        )

    def keep_output(m):
        return pltpu.make_async_copy(r["xout"].at[m], r["outputs"].at[0, m, 0], r["store"].at[m])

    def keep_gradient(m):
        return pltpu.make_async_copy(r["gout"].at[m], r["input_grads"].at[0, m, 0], r["store"].at[2 + m])

    @pl.when(is_first)
    def _():
        for m in range(2):
            entry(m).start()

    for load in loads:
        load.start()

    @pl.when(is_last)
    def _():
        for m in range(2):
            end_gradient(m).start()

    barrier = pltpu.get_barrier_semaphore()
    for neighbour in (before, after):
        pl.semaphore_signal(barrier, inc=1, device_id={"section": neighbour}, device_id_type=MESH)
    pl.semaphore_wait(barrier, 2)

    for load in loads:
        load.wait()

    @pl.when(jnp.logical_not(is_first))
    def _():
        transpose_weights(r)

    @pl.loop(0, 2)
    def _(m):
        @pl.when(is_first)
        def _():
            entry(m).wait()

        @pl.when(jnp.logical_not(is_first))
        def _():
            pass_on(m).wait_recv()

        forward_step(m, r)

        @pl.when(jnp.logical_not(is_last))
        def _():
            pass_on(m).start()

        keep_output(m).start()

    @pl.when(is_first)
    def _():
        transpose_weights(r)

    for m in range(2):
        r["normed_t"][:, 128 * m : 128 * m + 128] = r["normed"][m].T
        r["mixed_t"][:, 128 * m : 128 * m + 128] = r["mixed"][m].T

    @pl.loop(0, 2)
    def _(m):
        @pl.when(is_last)
        def _():
            end_gradient(m).wait()

        @pl.when(jnp.logical_not(is_last))
        def _():
            pass_back(m).wait_recv()

        backward_step(m, r)

        @pl.when(jnp.logical_not(is_first))
        def _():
            pass_back(m).start()

        keep_gradient(m).start()

    @pl.loop(0, 12)
    def _(j):
        c = pl.ds(pl.multiple_of(256 * j, 256), 256)
        r["part_qkv"][:, c] = dg(
            r["normed_t"][...], r["gproj"][:, :, c].reshape(256, 256)
        ).astype(BF16)

    @pl.loop(0, 4)
    def _(j):
        c = pl.ds(pl.multiple_of(256 * j, 256), 256)
        r["part_out"][:, c] = dg(
            r["mixed_t"][...], r["gin"][:, :, c].reshape(256, 256)
        ).astype(BF16)

    for m in range(2):
        keep_output(m).wait()
        keep_gradient(m).wait()

        @pl.when(jnp.logical_not(is_last))
        def _():
            pass_on(m).wait_send()

        @pl.when(jnp.logical_not(is_first))
        def _():
            pass_back(m).wait_send()


def relay(patches, segments, w_qkv, w_out, cotangent):
    inputs = [
        ("patches", patches, pl.ANY),
        ("segments", segments, pltpu.VMEM),
        ("w_qkv_hbm", w_qkv, pl.ANY),
        ("w_out_hbm", w_out, pl.ANY),
        ("cotangent", cotangent, pl.ANY),
    ]
    stacked = (1,) + patches.shape
    results = [
        ("outputs", stacked, BF16, pl.ANY),
        ("input_grads", stacked, BF16, pl.ANY),
        ("part_qkv", w_qkv.shape[1:], BF16, pltpu.VMEM),
        ("part_out", w_out.shape[1:], BF16, pltpu.VMEM),
    ]
    block = (2, 128, 1024)
    scratch = [
        ("xin", pltpu.VMEM(block, BF16)),
        ("gin", pltpu.VMEM(block, BF16)),
        ("xout", pltpu.VMEM(block, BF16)),
        ("gout", pltpu.VMEM(block, BF16)),
        ("normed", pltpu.VMEM(block, BF16)),
        ("mixed", pltpu.VMEM(block, BF16)),
        ("normed_t", pltpu.VMEM((1024, 256), BF16)),
        ("mixed_t", pltpu.VMEM((1024, 256), BF16)),
        ("gproj", pltpu.VMEM((2, 128, 3072), BF16)),
        ("gn", pltpu.VMEM((128, 1024), F32)),
        ("wqkv", pltpu.VMEM((1024, 3072), BF16)),
        ("wout", pltpu.VMEM((1024, 1024), BF16)),
        ("wqkv_t", pltpu.VMEM((3072, 1024), BF16)),
        ("wout_t", pltpu.VMEM((1024, 1024), BF16)),
        ("xinv", pltpu.VMEM((2, 128, 128), F32)),
        ("qs", pltpu.VMEM((2, 8, 128, 128), BF16)),
        ("kt", pltpu.VMEM((2, 8, 128, 128), BF16)),
        ("v", pltpu.VMEM((2, 8, 128, 128), BF16)),
        ("qi", pltpu.VMEM((2, 8, 2, 128), F32)),
        ("ki", pltpu.VMEM((2, 8, 2, 128), F32)),
        ("probs", pltpu.VMEM((2, 8, 128, 256), BF16)),
        ("load", pltpu.SemaphoreType.DMA((6,))),
        ("store", pltpu.SemaphoreType.DMA((4,))),
        ("x_send", pltpu.SemaphoreType.DMA((2,))),
        ("x_recv", pltpu.SemaphoreType.DMA((2,))),
        ("g_send", pltpu.SemaphoreType.DMA((2,))),
        ("g_recv", pltpu.SemaphoreType.DMA((2,))),
    ]
    names = [i[0] for i in inputs] + [o[0] for o in results] + [s[0] for s in scratch]
    return pl.pallas_call(
        functools.partial(relay_kernel, names),
        out_shape=[jax.ShapeDtypeStruct(o[1], o[2]) for o in results],
        in_specs=[pl.BlockSpec(memory_space=i[2]) for i in inputs],
        out_specs=[pl.BlockSpec(memory_space=o[3]) for o in results],
        scratch_shapes=[s[1] for s in scratch],
        compiler_params=pltpu.CompilerParams(
            collective_id=0, has_side_effects=True, vmem_limit_bytes=58 << 20
        ),
        name="relay",
    )(*[i[1] for i in inputs])


def on_device(patches, segment_ids, weights_qkv, weights_out, cotangent):
    produced, grads, whole_qkv, whole_out = relay(
        patches, segment_ids, weights_qkv, weights_out, cotangent
    )
    total_qkv = lax.psum_scatter(whole_qkv, "dp", scatter_dimension=0, tiled=True).astype(F32)
    total_out = lax.psum_scatter(whole_out, "dp", scatter_dimension=1, tiled=True).astype(F32)
    return (produced, grads, total_qkv[None], total_out[None])


def solution(mesh):
    return jax.shard_map(
        on_device,
        mesh=mesh,
        in_specs=(
            P(None, "dp", None, None),
            P(None, "dp", None),
            P("section", None, None),
            P("section", None, None),
            P(None, "dp", None, None),
        ),
        out_specs=(
            P("section", None, "dp", None, None),
            P("section", None, "dp", None, None),
            P("section", "dp", None),
            P("section", None, "dp"),
        ),
        check_vma=False,
    )
```

time: 495 us -> 286 us (0.58)
  the two profiles are of different devices: /device:TPU:0 before, /device:TPU:1 now
where the time goes in v1:
time: 286 us; the launch traced here: 284 us
  waiting for transfers between devices  167 us (58%)
  Pallas kernels  94.1 us (33%)
  between operations  14.1 us (5%)
  local copies, waits for them, and re-layouts  7.36 us (3%)
    pallas_call x1, Pallas kernels, relay(): pl.pallas_call(functools.partial(relay_kernel, names), out_shape=[jax.Sha...  94.1 us
    reduce_scatter x1, waiting for transfers between devices, on_device(): lax.psum_scatter(whole_qkv, 'dp', scatter_dimension=0, tiled=True)  87.4 us
    unnamed x3, waiting for transfers between devices  79.6 us
    unnamed x9, local copies, waits for them, and re-layouts  7.36 us
  transfers between devices with their start and end apart: 2, of which 2 were waited for; matrix products, arithmetic and copies ran while one was open for 1% of the time, Pallas kernels for 0%

profile of v1, /device:TPU:1, one launch (start us, length us, event | category | flops | bytes accessed | tf_op | source)
XLA Modules:
  0.0 284.4 jit_solution(5947011445803704881)
XLA Ops:
  7.2 0.0 reduce-scatter.7.cloned.1.call-start
  7.2 94.1 %relay.1 = (bf16[1,2,1,128,1024]{4,3,2,1,0:T(8,128)(2,1)}, bf16[1,2,1,128,1024]{4,3,2,1,0:T(8,128)(2,1)}, bf16[1024,3072]{1,0:T(8,128)(2,1)}, bf16[1024,1024]{1,0:T(8,128)(2,1)}) custom-call(bf16[2,1,128,1024]{3,2,1,0:T(8,128)(2,1)} %refs_0_.1, s32[2,1,128]{2,1,0:T(1,128)} %refs_1_.1, bf16[1,1024,3072]{2,1,0:T(8,128)(2,1)} %refs_2_.1, ...), custom_call_target="tpu_custom_call" | custom-call | tf_op jit(solution)/shard_map/relay/pallas_call | solution.py:297
  101.3 3.9 %copy.11 = bf16[1024,1024]{0,1:T(8,128)(2,1)} copy(bf16[1024,1024]{1,0:T(8,128)(2,1)} %get-tuple-element.11) | data formatting | bytes 4194304
  105.2 0.0 reduce-scatter.7.cloned.1.call-update
  105.3 0.0 reduce-scatter.5.cloned.1.call-start
  105.3 0.7 reduce-scatter.5.cloned.1.call-update
  106.0 0.0 copy-start.1
  106.0 0.0 copy-start
  106.0 78.9 %reduce-scatter.7.cloned.1.call-done = bf16[32,1024]{1,0:T(8,128)(2,1)} async-done(((bf16[1024,1024]{1,0:T(8,128)(2,1)}), bf16[32,1024]{1,0:T(8,128)(2,1)}) %reduce-scatter.7.cloned.1.call-update) | async-done | bytes 65552
  185.0 1.0 copy.12
  186.0 0.8 copy.10
  186.9 87.4 %reduce-scatter.5.cloned.1.call-done = bf16[32,3072]{1,0:T(8,128)(2,1)} async-done(((bf16[1024,3072]{1,0:T(8,128)(2,1)}), bf16[32,3072]{1,0:T(8,128)(2,1)}) %reduce-scatter.5.cloned.1.call-update) | async-done | bytes 196624 | tf_op jit(solution)/shard_map/reduce_scatter | solution.py:314
  274.3 1.7 bitcast_convert_fusion.1
  276.0 0.0 copy-done.1
  276.0 0.8 copy.15
  276.8 0.0 copy-done
  276.8 0.8 copy.16
  (1 shorter events, 0.0 us)
Async XLA Ops:
  7.2 177.8 %reduce-scatter.7.cloned.1.call-start = ((), (), s32[]{:S(2)}) async-start(), calls=%async_computation.3 | async-start | bytes 2162688
  105.3 169.0 %reduce-scatter.5.cloned.1.call-start = ((), (), s32[]{:S(2)}) async-start(), calls=%async_computation.2 | async-start | bytes 6488064 | tf_op jit(solution)/shard_map/reduce_scatter | solution.py:314
  106.0 170.0 %copy-start.1 = (bf16[1,2,1,128,1024]{4,3,2,1,0:T(8,128)(2,1)S(1)}, bf16[1,2,1,128,1024]{4,3,2,1,0:T(8,128)(2,1)}, u32[]{:S(2)}) copy-start(bf16[1,2,1,128,1024]{4,3,2,1,0:T(8,128)(2,1)} %get-tuple-element.24) | copy-start | bytes 1572868
  106.0 170.8 %copy-start = (bf16[1,2,1,128,1024]{4,3,2,1,0:T(8,128)(2,1)S(1)}, bf16[1,2,1,128,1024]{4,3,2,1,0:T(8,128)(2,1)}, u32[]{:S(2)}) copy-start(bf16[1,2,1,128,1024]{4,3,2,1,0:T(8,128)(2,1)} %get-tuple-element.25) | copy-start | bytes 1572868
Sparse Core Ops, SparseCore 0:
  105.4 79.5 reduce-scatter.6
  188.7 85.5 reduce-scatter.4

commit v2 on v1

v2 whole, which is shorter than its diff:
```python
import functools
import types

import jax
import jax.numpy as jnp
from jax import lax
from jax.experimental import pallas as pl
from jax.experimental.pallas import tpu as pltpu
from jax.sharding import PartitionSpec as P

BF16 = jnp.bfloat16
F32 = jnp.float32
EPSILON = 1e-6
MESH = pl.DeviceIdType.MESH


def dg(a,b,ca=1,cb=0): return lax.dot_general(a,b,(((ca,),(cb,)),((),())),preferred_element_type=F32)

def block_diagonal(pair):
    blank = jnp.zeros((64, pair.shape[1]), pair.dtype)
    top = jnp.concatenate([pair[:64], blank], axis=1)
    bottom = jnp.concatenate([blank, pair[64:]], axis=1)
    return jnp.concatenate([top, bottom], axis=0)

def head_norm(rows):
    grouped = rows.reshape(2, 64, rows.shape[1])
    centred = grouped - jnp.mean(grouped, axis=1, keepdims=True)
    inverse = lax.rsqrt(jnp.mean(centred * centred, axis=1, keepdims=True) + EPSILON)
    return (centred * inverse).reshape(rows.shape), inverse[:, 0, :]

def head_norm_pull(grad, normed, inverse):
    tokens = grad.shape[1]
    g = grad.reshape(2, 64, tokens)
    n = normed.reshape(2, 64, tokens)
    first = jnp.mean(g, axis=1, keepdims=True)
    second = jnp.mean(g * n, axis=1, keepdims=True)
    return ((g - first - n * second) * inverse[:, None, :]).reshape(grad.shape)

def normalise(m, r):
    x = r.xin[m].astype(F32)
    centred = x - jnp.mean(x, axis=-1, keepdims=True)
    inverse = lax.rsqrt(jnp.mean(centred * centred, axis=-1, keepdims=True) + EPSILON)
    r.xinv[m] = jnp.broadcast_to(inverse, (128, 128))
    r.normed[m] = (centred * inverse).astype(BF16)


def attend(m, r):
    queries_in = jnp.broadcast_to(r.segments[m].astype(F32), (128, 128))
    allowed = queries_in == queries_in.T
    allowed = jnp.concatenate([allowed, allowed], axis=1)
    normed = r.normed[m]
    live = {}

    def project(quad):
        for name, start in (("q", 0), ("k", 1024), ("v", 2048)):
            column = start + 256 * quad
            live[name, quad] = dg(normed, r.wqkv[:, column : column + 256])

    def norms(quad):
        for half in range(2):
            pair = 2 * quad + half
            c = slice(128 * half, 128 * half + 128)
            q, r.qi[m, pair] = head_norm(live["q", quad][:, c].T)
            k, r.ki[m, pair] = head_norm(live["k", quad][:, c].T)
            v = live["v", quad][:, c].astype(BF16)
            qs, kt = (q * 0.125).astype(BF16), k.astype(BF16)
            r.qs[m, pair], r.kt[m, pair], r.v[m, pair] = qs, kt, v
            live["qs", pair], live["kn", pair], live["vt", pair] = qs, kt.T, v.T

    def scores(quad):
        for pair in (2 * quad, 2 * quad + 1):
            live["s", pair] = dg(live["kn", pair], block_diagonal(live["qs", pair]))

    def softmax(quad):
        for pair in (2 * quad, 2 * quad + 1):
            w = jnp.where(allowed, jnp.exp(live["s", pair]), 0.0)
            p = (w * (1.0 / jnp.sum(w, axis=0, keepdims=True))).astype(BF16)
            r.probs[m, pair] = p
            live["p", pair] = p

    def mix(quad):
        for pair in (2 * quad, 2 * quad + 1):
            vt, p = live["vt", pair], live["p", pair]
            o = [dg(vt[64 * i : 64 * i + 64], p[:, 128 * i : 128 * i + 128]) for i in range(2)]
            live["o", pair] = jnp.concatenate(o, axis=0).astype(BF16)

    def turn(quad):
        for pair in (2 * quad, 2 * quad + 1):
            r.mixed[m, :, 128 * pair : 128 * pair + 128] = live["o", pair].T

    for stage in (project, norms, scores, softmax, mix, turn):
        for quad in range(4):
            stage(quad)


def project_out(m, r):
    mixed = r.mixed[m]
    for j in range(4):
        c = slice(256*j, 256*j+256)
        branch = dg(mixed, r.wout[:, c])
        r.xout[m, :, c] = (r.xin[m, :, c].astype(F32) + branch).astype(BF16)

def attend_pull(m, r):
    g = r.gin[m]
    live = {}

    def project(quad):
        go4 = dg(g, r.wout_t[:, 256 * quad : 256 * quad + 256]).astype(BF16)
        for half in range(2):
            live["go", 2 * quad + half] = go4[:, 128 * half : 128 * half + 128].T

    def probs_pull(quad):
        for pair in (2 * quad, 2 * quad + 1):
            live["dp", pair] = dg(r.v[m, pair], block_diagonal(live["go", pair]))

    def values_pull(quad):
        for pair in (2 * quad, 2 * quad + 1):
            go, p = live["go", pair], r.probs[m, pair]
            gv = [dg(go[64 * i : 64 * i + 64], p[:, 128 * i : 128 * i + 128], 1, 1) for i in range(2)]
            live["gv", pair] = jnp.concatenate(gv, axis=0).astype(BF16)

    def scores_pull(quad):
        for pair in (2 * quad, 2 * quad + 1):
            p = r.probs[m, pair].astype(F32)
            pd = p * live["dp", pair]
            live["ds", pair] = (pd - p * jnp.sum(pd, axis=0, keepdims=True)).astype(BF16)

    def heads_pull(quad):
        for pair in (2 * quad, 2 * quad + 1):
            ds, kt, qs = live["ds", pair], r.kt[m, pair], r.qs[m, pair]
            cut = [(slice(64 * i, 64 * i + 64), slice(128 * i, 128 * i + 128)) for i in range(2)]
            live["gq", pair] = jnp.concatenate([dg(kt[i], ds[:, c]) for i, c in cut], axis=0)
            live["gk", pair] = jnp.concatenate([dg(qs[i], ds[:, c], 1, 1) for i, c in cut], axis=0)

    def norms_pull(quad):
        for pair in (2 * quad, 2 * quad + 1):
            qs, kt = r.qs[m, pair].astype(F32), r.kt[m, pair].astype(F32)
            gq = head_norm_pull(live["gq", pair] * 0.125, qs * 8.0, r.qi[m, pair])
            gk = head_norm_pull(live["gk", pair], kt, r.ki[m, pair])
            live["gq", pair], live["gk", pair] = gq.astype(BF16), gk.astype(BF16)

    def turn(quad):
        for pair in (2 * quad, 2 * quad + 1):
            for name, start in (("gq", 0), ("gk", 1024), ("gv", 2048)):
                column = start + 128 * pair
                r.gproj[m, :, column : column + 128] = live[name, pair].T

    for stage in (project, probs_pull, scores_pull, values_pull, heads_pull, norms_pull, turn):
        for quad in range(4):
            stage(quad)


def input_pull(m, r):
    gproj = r.gproj[m]
    for j in range(4):
        r.gn[:, 256*j:256*j+256] = dg(gproj, r.wqkv_t[:, 256*j:256*j+256])
    gn = r.gn[...]
    n = r.normed[m].astype(F32)
    first = jnp.mean(gn, axis=-1, keepdims=True)
    second = jnp.mean(gn * n, axis=-1, keepdims=True)
    dx = (gn - first - n * second) * r.xinv[m][:, :1]
    r.gout[m] = (r.gin[m].astype(F32) + dx).astype(BF16)

def transpose_weights(r):
    for j in range(8):
        r.wqkv_t[:, 128*j:128*j+128] = r.wqkv[128*j:128*j+128, :].T
        r.wout_t[:, 128*j:128*j+128] = r.wout[128*j:128*j+128, :].T


def spread(r, name, column, rows):
    getattr(r, name)[:, :, :, column : column + 128] = rows.T.reshape(16, 2, 32, 128)


def relay_kernel(names, *refs):
    r = types.SimpleNamespace(**dict(zip(names, refs)))
    section = lax.axis_index("section")
    last = lax.axis_size("section") - 1
    after = lax.rem(section + 1, last + 1)
    before = lax.rem(section + last, last + 1)
    is_first = section == 0
    is_last = section == last
    place = lax.axis_index("dp")
    core = lax.rem(place, 2)
    z = lax.rem(place // 2, 4)
    y = place // 8
    partner = place + 1 - 2 * core
    y_peers = [place + 8 * (lax.rem(y + k, 4) - y) for k in (1, 2, 3)]
    z_peers = [place + 2 * (lax.rem(z + k, 4) - z) for k in (1, 2, 3)]
    early = jnp.logical_or(jnp.logical_not(is_first), core == 1)

    loads = [
        pltpu.make_async_copy(r.w_qkv_hbm.at[0], r.wqkv, r.load.at[0]),
        pltpu.make_async_copy(r.w_out_hbm.at[0], r.wout, r.load.at[1]),
    ]

    def entry(m):
        return pltpu.make_async_copy(r.patches.at[m, 0], r.xin.at[m], r.load.at[2 + m])

    def end_gradient(m):
        return pltpu.make_async_copy(r.cotangent.at[m, 0], r.gin.at[m], r.load.at[4 + m])

    def pass_on(m):
        return pltpu.make_async_remote_copy(
            src_ref=r.xout.at[m], dst_ref=r.xin.at[m],
            send_sem=r.x_send.at[m], recv_sem=r.x_recv.at[m],
            device_id={"section": after}, device_id_type=MESH,
        )

    def pass_back(m):
        return pltpu.make_async_remote_copy(
            src_ref=r.gout.at[m], dst_ref=r.gin.at[m],
            send_sem=r.g_send.at[m], recv_sem=r.g_recv.at[m],
            device_id={"section": before}, device_id_type=MESH,
        )

    def keep_output(m):
        return pltpu.make_async_copy(r.xout.at[m], r.outputs.at[0, m, 0], r.store.at[m])

    def keep_gradient(m):
        return pltpu.make_async_copy(r.gout.at[m], r.input_grads.at[0, m, 0], r.store.at[2 + m])

    def share(name, m, index):
        return pltpu.make_async_remote_copy(
            src_ref=getattr(r, name).at[m], dst_ref=getattr(r, "their_" + name).at[m],
            send_sem=r.share_send.at[index, m], recv_sem=r.share_recv.at[index, m],
            device_id={"dp": partner}, device_id_type=MESH,
        )

    shared = ["normed", "mixed", "gin", "gproj"]

    def first_sum(half, j, k):
        if half == 0:
            block, peer = r.part.at[0, j, lax.rem(y + k, 4)], y_peers[k - 1]
        else:
            block, peer = r.part.at[1, j, :, lax.rem(z + k, 4)], z_peers[k - 1]
        return pltpu.make_async_remote_copy(
            src_ref=block, dst_ref=r.first.at[half, j, k - 1],
            send_sem=r.first_send.at[half, j, k - 1], recv_sem=r.first_recv.at[half, j, k - 1],
            device_id={"dp": peer}, device_id_type=MESH,
        )

    def second_sum(half, j, k):
        if half == 0:
            block, peer = r.half_sum.at[0, j, lax.rem(z + k, 4)], z_peers[k - 1]
        else:
            block, peer = r.half_sum.at[1, j, lax.rem(y + k, 4)], y_peers[k - 1]
        return pltpu.make_async_remote_copy(
            src_ref=block, dst_ref=r.second.at[half, j, k - 1],
            send_sem=r.second_send.at[half, j, k - 1], recv_sem=r.second_recv.at[half, j, k - 1],
            device_id={"dp": peer}, device_id_type=MESH,
        )

    @pl.when(is_first)
    def _():
        for m in range(2):
            entry(m).start()

    for load in loads:
        load.start()

    @pl.when(is_last)
    def _():
        for m in range(2):
            end_gradient(m).start()

    barrier = pltpu.get_barrier_semaphore()
    for neighbour in (before, after):
        pl.semaphore_signal(barrier, inc=1, device_id={"section": neighbour}, device_id_type=MESH)
    for peer in [partner] + y_peers + z_peers:
        pl.semaphore_signal(barrier, inc=1, device_id={"dp": peer}, device_id_type=MESH)

    @pl.when(early)
    def _():
        for load in loads:
            load.wait()
        transpose_weights(r)

    @pl.loop(0, 2)
    def _(m):
        @pl.when(is_first)
        def _():
            entry(m).wait()

        @pl.when(jnp.logical_not(is_first))
        def _():
            pass_on(m).wait_recv()

        normalise(m, r)

        @pl.when(jnp.logical_and(m == 0, jnp.logical_not(early)))
        def _():
            for load in loads:
                load.wait()

        attend(m, r)
        project_out(m, r)

        @pl.when(m == 0)
        def _():
            pl.semaphore_wait(barrier, 9)

        @pl.when(jnp.logical_not(is_last))
        def _():
            pass_on(m).start()

        keep_output(m).start()
        share("normed", m, 0).start()
        share("mixed", m, 1).start()

    @pl.when(jnp.logical_not(early))
    def _():
        transpose_weights(r)

    for m in range(2):
        share("normed", m, 0).wait_recv()
        share("mixed", m, 1).wait_recv()
    for m in range(2):
        spread(r, "normed_t", 128 * m, r.normed[m])
        spread(r, "normed_t", 256 + 128 * m, r.their_normed[m])

    @pl.loop(0, 2)
    def _(m):
        @pl.when(is_last)
        def _():
            end_gradient(m).wait()

        @pl.when(jnp.logical_not(is_last))
        def _():
            pass_back(m).wait_recv()

        share("gin", m, 2).start()
        attend_pull(m, r)
        share("gproj", m, 3).start()

        @pl.when(jnp.logical_not(is_first))
        def _():
            input_pull(m, r)
            pass_back(m).start()
            keep_gradient(m).start()

    for m in range(2):
        share("gproj", m, 3).wait_recv()

    def partial(half, j):
        column = 2048 * half + 512 * j
        if column < 3072:
            rows, name, c = r.normed_t, "gproj", slice(column, column + 512)
        else:
            rows, name, c = r.gin_t, "mixed", slice(column - 3072, column - 2560)
        rows = rows[:, core].reshape(512, 512)
        total = dg(rows[:, :256], getattr(r, name)[:, :, c].reshape(256, 512))
        total = total + dg(rows[:, 256:], getattr(r, "their_" + name)[:, :, c].reshape(256, 512))
        r.part[half, j] = total.astype(BF16).reshape(4, 4, 32, 512)

    pieces = [(half, j) for j in range(4) for half in range(2)]
    for half, j in pieces:
        if (half, j) == (1, 2):
            for m in range(2):
                share("gin", m, 2).wait_recv()
                spread(r, "gin_t", 128 * m, r.gin[m])
                spread(r, "gin_t", 256 + 128 * m, r.their_gin[m])
        partial(half, j)
        for k in (1, 2, 3):
            first_sum(half, j, k).start()

    @pl.when(is_first)
    def _():
        @pl.loop(0, 2)
        def _(m):
            input_pull(m, r)
            keep_gradient(m).start()

    for half, j in pieces:
        for k in (1, 2, 3):
            first_sum(half, j, k).wait_recv()
        own = r.part[half, j, y] if half == 0 else r.part[half, j, :, z]
        total = own.astype(F32)
        for k in (1, 2, 3):
            total = total + r.first[half, j, k - 1].astype(F32)
        r.half_sum[half, j] = total.astype(BF16)
        for k in (1, 2, 3):
            second_sum(half, j, k).start()

    for half, j in pieces:
        for k in (1, 2, 3):
            second_sum(half, j, k).wait_recv()
        total = r.half_sum[half, j, z if half == 0 else y].astype(F32)
        for k in (1, 2, 3):
            total = total + r.second[half, j, k - 1].astype(F32)
        column = 2048 * half + 512 * j
        if column < 3072:
            r.total_qkv[0, :, column : column + 512] = total
        else:
            r.total_out_t[:, column - 3072 : column - 2560] = total

    for half, j in pieces:
        for k in (1, 2, 3):
            first_sum(half, j, k).wait_send()
            second_sum(half, j, k).wait_send()
    for index, name in enumerate(shared):
        for m in range(2):
            share(name, m, index).wait_send()

    for m in range(2):
        keep_output(m).wait()
        keep_gradient(m).wait()

        @pl.when(jnp.logical_not(is_last))
        def _():
            pass_on(m).wait_send()

        @pl.when(jnp.logical_not(is_first))
        def _():
            pass_back(m).wait_send()


def relay(patches, segments, w_qkv, w_out, cotangent):
    inputs = [
        ("patches", patches, pl.ANY),
        ("segments", segments, pltpu.VMEM),
        ("w_qkv_hbm", w_qkv, pl.ANY),
        ("w_out_hbm", w_out, pl.ANY),
        ("cotangent", cotangent, pl.ANY),
    ]
    stacked = (1,) + patches.shape
    results = [
        ("outputs", stacked, BF16, pl.ANY),
        ("input_grads", stacked, BF16, pl.ANY),
        ("total_qkv", (1, 32, 3072), F32, pltpu.VMEM),
        ("total_out_t", (32, 1024), F32, pltpu.VMEM),
    ]
    block = (2, 128, 1024)
    scratch = [
        ("xin", pltpu.VMEM(block, BF16)),
        ("gin", pltpu.VMEM(block, BF16)),
        ("xout", pltpu.VMEM(block, BF16)),
        ("gout", pltpu.VMEM(block, BF16)),
        ("normed", pltpu.VMEM(block, BF16)),
        ("mixed", pltpu.VMEM(block, BF16)),
        ("their_normed", pltpu.VMEM(block, BF16)),
        ("their_mixed", pltpu.VMEM(block, BF16)),
        ("their_gin", pltpu.VMEM(block, BF16)),
        ("their_gproj", pltpu.VMEM((2, 128, 3072), BF16)),
        ("normed_t", pltpu.VMEM((16, 2, 32, 512), BF16)),
        ("gin_t", pltpu.VMEM((16, 2, 32, 512), BF16)),
        ("part", pltpu.VMEM((2, 4, 4, 4, 32, 512), BF16)),
        ("first", pltpu.VMEM((2, 4, 3, 4, 32, 512), BF16)),
        ("half_sum", pltpu.VMEM((2, 4, 4, 32, 512), BF16)),
        ("second", pltpu.VMEM((2, 4, 3, 32, 512), BF16)),
        ("share_send", pltpu.SemaphoreType.DMA((4, 2))),
        ("share_recv", pltpu.SemaphoreType.DMA((4, 2))),
        ("first_send", pltpu.SemaphoreType.DMA((2, 4, 3))),
        ("first_recv", pltpu.SemaphoreType.DMA((2, 4, 3))),
        ("second_send", pltpu.SemaphoreType.DMA((2, 4, 3))),
        ("second_recv", pltpu.SemaphoreType.DMA((2, 4, 3))),
        ("gproj", pltpu.VMEM((2, 128, 3072), BF16)),
        ("gn", pltpu.VMEM((128, 1024), F32)),
        ("wqkv", pltpu.VMEM((1024, 3072), BF16)),
        ("wout", pltpu.VMEM((1024, 1024), BF16)),
        ("wqkv_t", pltpu.VMEM((3072, 1024), BF16)),
        ("wout_t", pltpu.VMEM((1024, 1024), BF16)),
        ("xinv", pltpu.VMEM((2, 128, 128), F32)),
        ("qs", pltpu.VMEM((2, 8, 128, 128), BF16)),
        ("kt", pltpu.VMEM((2, 8, 128, 128), BF16)),
        ("v", pltpu.VMEM((2, 8, 128, 128), BF16)),
        ("qi", pltpu.VMEM((2, 8, 2, 128), F32)),
        ("ki", pltpu.VMEM((2, 8, 2, 128), F32)),
        ("probs", pltpu.VMEM((2, 8, 128, 256), BF16)),
        ("load", pltpu.SemaphoreType.DMA((6,))),
        ("store", pltpu.SemaphoreType.DMA((4,))),
        ("x_send", pltpu.SemaphoreType.DMA((2,))),
        ("x_recv", pltpu.SemaphoreType.DMA((2,))),
        ("g_send", pltpu.SemaphoreType.DMA((2,))),
        ("g_recv", pltpu.SemaphoreType.DMA((2,))),
    ]
    names = [i[0] for i in inputs] + [o[0] for o in results] + [s[0] for s in scratch]
    return pl.pallas_call(
        functools.partial(relay_kernel, names),
        out_shape=[jax.ShapeDtypeStruct(o[1], o[2]) for o in results],
        in_specs=[pl.BlockSpec(memory_space=i[2]) for i in inputs],
        out_specs=[pl.BlockSpec(memory_space=o[3]) for o in results],
        scratch_shapes=[s[1] for s in scratch],
        compiler_params=pltpu.CompilerParams(
            collective_id=0, has_side_effects=True, vmem_limit_bytes=58 << 20
        ),
        name="relay",
    )(*[i[1] for i in inputs])


def settle_kernel(count, *refs):
    sources, targets, held = refs[:count], refs[count : 2 * count], refs[2 * count : 3 * count]
    read, written = refs[-2:]
    into = [pltpu.make_async_copy(a, b, read.at[i]) for i, (a, b) in enumerate(zip(sources, held))]
    out = [pltpu.make_async_copy(a, b, written.at[i]) for i, (a, b) in enumerate(zip(held, targets))]
    for copy in into:
        copy.start()
    for first, second in zip(into, out):
        first.wait()
        second.start()
    for copy in out:
        copy.wait()


def settle(arrays):
    return pl.pallas_call(
        functools.partial(settle_kernel, len(arrays)),
        out_shape=[jax.ShapeDtypeStruct(a.shape, a.dtype) for a in arrays],
        in_specs=[pl.BlockSpec(memory_space=pl.ANY)] * len(arrays),
        out_specs=[pl.BlockSpec(memory_space=pl.ANY)] * len(arrays),
        scratch_shapes=[pltpu.VMEM(a.shape, a.dtype) for a in arrays]
        + [pltpu.SemaphoreType.DMA((len(arrays),))] * 2,
        name="settle",
    )(*arrays)


def on_device(patches, segment_ids, weights_qkv, weights_out, cotangent):
    produced, grads, total_qkv, total_out_t = settle(
        relay(patches, segment_ids, weights_qkv, weights_out, cotangent)
    )
    return (produced, grads, total_qkv, total_out_t.T[None])


def solution(mesh):
    return jax.shard_map(
        on_device,
        mesh=mesh,
        in_specs=(
            P(None, "dp", None, None),
            P(None, "dp", None),
            P("section", None, None),
            P("section", None, None),
            P(None, "dp", None, None),
        ),
        out_specs=(
            P("section", None, "dp", None, None),
            P("section", None, "dp", None, None),
            P("section", "dp", None),
            P("section", None, "dp"),
        ),
        check_vma=False,
    )
```

time: 286 us -> 124 us (0.43)
  waiting for transfers between devices: 167 us -> 0 us
  Pallas kernels: 94.1 us -> 123 us
  between operations: 14.1 us -> 0.8 us
  local copies, waits for them, and re-layouts: 7.36 us -> 0 us
    reduce_scatter x1 -> x0, waiting for transfers between devices: 87.4 us -> none  [on_device(): lax.psum_scatter(whole_qkv, 'dp', scatter_dimension=0, tiled=True)]
    unnamed x3 -> x0, waiting for transfers between devices: 79.6 us -> none
    pallas_call x1, Pallas kernels: 94.1 us -> 121 us  [relay(): pl.pallas_call(functools.partial(relay_kernel, names), out_shape=[jax.Sha...]
    unnamed x9 -> x0, local copies, waits for them, and re-layouts: 7.36 us -> none
  transfers between devices with their start and end apart: 2 -> 0, of which waited for: 2 -> 0; matrix products, arithmetic and copies ran while one was open for 1% -> 0% of each run, Pallas kernels for 0% -> 0%
where the time goes in v2:
time: 124 us
  Pallas kernels  123 us (99%)
    pallas_call x1, Pallas kernels, relay(): pl.pallas_call(functools.partial(relay_kernel, names), out_shape=[jax.Sha...  121 us

profile of v2, /device:TPU:1, one launch (start us, length us, event | category | flops | bytes accessed | tf_op | source)
XLA Modules:
  0.0 123.6 jit_solution(2947758223470188109)
XLA Ops:
  0.6 120.5 %relay.1 = (bf16[1,2,1,128,1024]{4,3,2,1,0:T(8,128)(2,1)}, bf16[1,2,1,128,1024]{4,3,2,1,0:T(8,128)(2,1)}, f32[1,32,3072]{2,1,0:T(8,128)}, f32[32,1024]{1,0:T(8,128)}) custom-call(bf16[2,1,128,1024]{3,2,1,0:T(8,128)(2,1)} %refs_0_.1, s32[2,1,128]{2,1,0:T(1,128)} %refs_1_.1, bf16[1,1024,3072]{2,1,0:T(8,128)(2,1)} %refs_2_.1, bf16[1,1024,1024]{2,1,0:T(8,128)(2,1)} %refs_3_.1, ...), custom_call_target="tpu_custom_call" | custom-call | tf_op jit(solution)/shard_map/relay/pallas_call | solution.py:477
  121.2 2.2 %settle.1 = (bf16[1,2,1,128,1024]{4,3,2,1,0:T(8,128)(2,1)}, bf16[1,2,1,128,1024]{4,3,2,1,0:T(8,128)(2,1)}, f32[1,32,3072]{2,1,0:T(8,128)}, f32[32,1024]{1,0:T(8,128)}) custom-call(bf16[1,2,1,128,1024]{4,3,2,1,0:T(8,128)(2,1)} %get-tuple-element.12.refs_0_, bf16[1,2,1,128,1024]{4,3,2,1,0:T(8,128)(2,1)} %get-tuple-element.13.refs_1_, ...), custom_call_target="tpu_custom_call" | custom-call | tf_op jit(solution)/shard_map/settle/pallas_call | solution.py:505

commit v3 on v2

--- a/solution.py
+++ b/solution.py
@@ -169,6 +169,14 @@
 
 def spread(r, name, column, rows):
     getattr(r, name)[:, :, :, column : column + 128] = rows.T.reshape(16, 2, 32, 128)
+
+
+def swap(p, mask):
+    if mask == 1:
+        return p + 1 - 2 * lax.rem(p, 2)
+    if mask == 2:
+        return lax.rem(p + 2, 4)
+    return 3 - p
 
 
 def relay_kernel(names, *refs):
@@ -184,8 +192,8 @@
     z = lax.rem(place // 2, 4)
     y = place // 8
     partner = place + 1 - 2 * core
-    y_peers = [place + 8 * (lax.rem(y + k, 4) - y) for k in (1, 2, 3)]
-    z_peers = [place + 2 * (lax.rem(z + k, 4) - z) for k in (1, 2, 3)]
+    y_peers = {a: place + 8 * (swap(y, a) - y) for a in (1, 3)}
+    z_peers = {a: place + 2 * (swap(z, a) - z) for a in (1, 3)}
     early = jnp.logical_or(jnp.logical_not(is_first), core == 1)
 
     loads = [
@@ -228,27 +236,70 @@
 
     shared = ["normed", "mixed", "gin", "gproj"]
 
-    def first_sum(half, j, k):
-        if half == 0:
-            block, peer = r.part.at[0, j, lax.rem(y + k, 4)], y_peers[k - 1]
+    def axes(half):
+        return ((y, y_peers), (z, z_peers)) if half == 0 else ((z, z_peers), (y, y_peers))
+
+    def masks(j):
+        return (1, 3) if j % 2 == 0 else (3, 1)
+
+    def block(half, j, position):
+        return r.part.at[0, j, position] if half == 0 else r.part.at[1, j, :, position]
+
+    def send(half, j, step):
+        (p, p_peers), (q, q_peers) = axes(half)
+        a, b = masks(j)
+        if step == 0:
+            source, target, peer = block(half, j, swap(p, 2)), r.far_in, p_peers[a]
+        elif step == 1:
+            source, target, peer = block(half, j, swap(p, a)), r.near_in, p_peers[a]
+        elif step == 2:
+            source, target, peer = r.far_sum.at[half, j], r.last_in, p_peers[b]
+        elif step == 3:
+            source, target, peer = r.row.at[half, j, swap(q, 2)], r.row_far_in, q_peers[a]
+        elif step == 4:
+            source, target, peer = r.row.at[half, j, swap(q, a)], r.row_near_in, q_peers[a]
         else:
-            block, peer = r.part.at[1, j, :, lax.rem(z + k, 4)], z_peers[k - 1]
+            source, target, peer = r.row_far_sum.at[half, j], r.row_last_in, q_peers[b]
         return pltpu.make_async_remote_copy(
-            src_ref=block, dst_ref=r.first.at[half, j, k - 1],
-            send_sem=r.first_send.at[half, j, k - 1], recv_sem=r.first_recv.at[half, j, k - 1],
+            src_ref=source, dst_ref=target.at[half, j],
+            send_sem=r.sum_send.at[half, j, step], recv_sem=r.sum_recv.at[half, j, step],
             device_id={"dp": peer}, device_id_type=MESH,
         )
 
-    def second_sum(half, j, k):
-        if half == 0:
-            block, peer = r.half_sum.at[0, j, lax.rem(z + k, 4)], z_peers[k - 1]
+    def sum_one(half, j):
+        (p, _), _ = axes(half)
+        send(half, j, 0).wait_recv()
+        held = block(half, j, swap(p, masks(j)[1]))[...].astype(F32)
+        r.far_sum[half, j] = (held + r.far_in[half, j].astype(F32)).astype(BF16)
+        send(half, j, 2).start()
+
+    def sum_two(half, j):
+        (p, _), _ = axes(half)
+        send(half, j, 1).wait_recv()
+        send(half, j, 2).wait_recv()
+        total = block(half, j, p)[...].astype(F32) + r.near_in[half, j].astype(F32)
+        r.row[half, j] = (total + r.last_in[half, j].astype(F32)).astype(BF16)
+        send(half, j, 3).start()
+        send(half, j, 4).start()
+
+    def sum_three(half, j):
+        _, (q, _) = axes(half)
+        send(half, j, 3).wait_recv()
+        held = r.row[half, j, swap(q, masks(j)[1])].astype(F32)
+        r.row_far_sum[half, j] = (held + r.row_far_in[half, j].astype(F32)).astype(BF16)
+        send(half, j, 5).start()
+
+    def sum_four(half, j):
+        _, (q, _) = axes(half)
+        send(half, j, 4).wait_recv()
+        send(half, j, 5).wait_recv()
+        total = r.row[half, j, q].astype(F32) + r.row_near_in[half, j].astype(F32)
+        total = total + r.row_last_in[half, j].astype(F32)
+        column = 2048 * half + 512 * j
+        if column < 3072:
+            r.total_qkv[0, :, column : column + 512] = total
         else:
-            block, peer = r.half_sum.at[1, j, lax.rem(y + k, 4)], y_peers[k - 1]
-        return pltpu.make_async_remote_copy(
-            src_ref=block, dst_ref=r.second.at[half, j, k - 1],
-            send_sem=r.second_send.at[half, j, k - 1], recv_sem=r.second_recv.at[half, j, k - 1],
-            device_id={"dp": peer}, device_id_type=MESH,
-        )
+            r.total_out_t[:, column - 3072 : column - 2560] = total
 
     @pl.when(is_first)
     def _():
@@ -266,7 +317,7 @@
     barrier = pltpu.get_barrier_semaphore()
     for neighbour in (before, after):
         pl.semaphore_signal(barrier, inc=1, device_id={"section": neighbour}, device_id_type=MESH)
-    for peer in [partner] + y_peers + z_peers:
+    for peer in [partner, *y_peers.values(), *z_peers.values()]:
         pl.semaphore_signal(barrier, inc=1, device_id={"dp": peer}, device_id_type=MESH)
 
     @pl.when(early)
@@ -275,8 +326,7 @@
             load.wait()
         transpose_weights(r)
 
-    @pl.loop(0, 2)
-    def _(m):
+    def forward(m):
         @pl.when(is_first)
         def _():
             entry(m).wait()
@@ -297,7 +347,7 @@
 
         @pl.when(m == 0)
         def _():
-            pl.semaphore_wait(barrier, 9)
+            pl.semaphore_wait(barrier, 7)
 
         @pl.when(jnp.logical_not(is_last))
         def _():
@@ -307,19 +357,23 @@
         share("normed", m, 0).start()
         share("mixed", m, 1).start()
 
-    @pl.when(jnp.logical_not(early))
-    def _():
-        transpose_weights(r)
-
-    for m in range(2):
-        share("normed", m, 0).wait_recv()
-        share("mixed", m, 1).wait_recv()
-    for m in range(2):
-        spread(r, "normed_t", 128 * m, r.normed[m])
-        spread(r, "normed_t", 256 + 128 * m, r.their_normed[m])
-
-    @pl.loop(0, 2)
-    def _(m):
+    def spread_normed():
+        for m in range(2):
+            share("normed", m, 0).wait_recv()
+            share("mixed", m, 1).wait_recv()
+        for m in range(2):
+            spread(r, "normed_t", 128 * m, r.normed[m])
+            spread(r, "normed_t", 256 + 128 * m, r.their_normed[m])
+
+    def backward(m):
+        @pl.when(jnp.logical_and(m == 0, jnp.logical_not(early)))
+        def _():
+            transpose_weights(r)
+
+        @pl.when(jnp.logical_and(m == 0, is_first))
+        def _():
+            spread_normed()
+
         @pl.when(is_last)
         def _():
             end_gradient(m).wait()
@@ -337,6 +391,25 @@
             input_pull(m, r)
             pass_back(m).start()
             keep_gradient(m).start()
+
+    turns = section // last
+
+    @pl.loop(0, 4)
+    def _(t):
+        back = turns * lax.rem(t, 2) + (1 - turns) * (t // 2)
+        m = turns * (t // 2) + (1 - turns) * lax.rem(t, 2)
+
+        @pl.when(back == 0)
+        def _():
+            forward(m)
+
+        @pl.when(back == 1)
+        def _():
+            backward(m)
+
+    @pl.when(jnp.logical_not(is_first))
+    def _():
+        spread_normed()
 
     for m in range(2):
         share("gproj", m, 3).wait_recv()
@@ -360,8 +433,8 @@
                 spread(r, "gin_t", 128 * m, r.gin[m])
                 spread(r, "gin_t", 256 + 128 * m, r.their_gin[m])
         partial(half, j)
-        for k in (1, 2, 3):
-            first_sum(half, j, k).start()
+        send(half, j, 0).start()
+        send(half, j, 1).start()
 
     @pl.when(is_first)
     def _():
@@ -370,33 +443,16 @@
             input_pull(m, r)
             keep_gradient(m).start()
 
+    stages = (sum_one, sum_two, sum_three, sum_four)
+    lags = (0, 3, 6, 9)
+    for step in range(len(pieces) + lags[-1]):
+        for lag, stage in zip(lags, stages):
+            if 0 <= step - lag < len(pieces):
+                stage(*pieces[step - lag])
+
     for half, j in pieces:
-        for k in (1, 2, 3):
-            first_sum(half, j, k).wait_recv()
-        own = r.part[half, j, y] if half == 0 else r.part[half, j, :, z]
-        total = own.astype(F32)
-        for k in (1, 2, 3):
-            total = total + r.first[half, j, k - 1].astype(F32)
-        r.half_sum[half, j] = total.astype(BF16)
-        for k in (1, 2, 3):
-            second_sum(half, j, k).start()
-
-    for half, j in pieces:
-        for k in (1, 2, 3):
-            second_sum(half, j, k).wait_recv()
-        total = r.half_sum[half, j, z if half == 0 else y].astype(F32)
-        for k in (1, 2, 3):
-            total = total + r.second[half, j, k - 1].astype(F32)
-        column = 2048 * half + 512 * j
-        if column < 3072:
-            r.total_qkv[0, :, column : column + 512] = total
-        else:
-            r.total_out_t[:, column - 3072 : column - 2560] = total
-
-    for half, j in pieces:
-        for k in (1, 2, 3):
-            first_sum(half, j, k).wait_send()
-            second_sum(half, j, k).wait_send()
+        for step in range(6):
+            send(half, j, step).wait_send()
     for index, name in enumerate(shared):
         for m in range(2):
             share(name, m, index).wait_send()
@@ -444,15 +500,12 @@
         ("normed_t", pltpu.VMEM((16, 2, 32, 512), BF16)),
         ("gin_t", pltpu.VMEM((16, 2, 32, 512), BF16)),
         ("part", pltpu.VMEM((2, 4, 4, 4, 32, 512), BF16)),
-        ("first", pltpu.VMEM((2, 4, 3, 4, 32, 512), BF16)),
-        ("half_sum", pltpu.VMEM((2, 4, 4, 32, 512), BF16)),
-        ("second", pltpu.VMEM((2, 4, 3, 32, 512), BF16)),
+        *((name, pltpu.VMEM((2, 4, 4, 32, 512), BF16)) for name in ("far_in", "near_in", "far_sum", "last_in", "row")),
+        *((name, pltpu.VMEM((2, 4, 32, 512), BF16)) for name in ("row_far_in", "row_near_in", "row_far_sum", "row_last_in")),
+        ("sum_send", pltpu.SemaphoreType.DMA((2, 4, 6))),
+        ("sum_recv", pltpu.SemaphoreType.DMA((2, 4, 6))),
         ("share_send", pltpu.SemaphoreType.DMA((4, 2))),
         ("share_recv", pltpu.SemaphoreType.DMA((4, 2))),
-        ("first_send", pltpu.SemaphoreType.DMA((2, 4, 3))),
-        ("first_recv", pltpu.SemaphoreType.DMA((2, 4, 3))),
-        ("second_send", pltpu.SemaphoreType.DMA((2, 4, 3))),
-        ("second_recv", pltpu.SemaphoreType.DMA((2, 4, 3))),
         ("gproj", pltpu.VMEM((2, 128, 3072), BF16)),
         ("gn", pltpu.VMEM((128, 1024), F32)),
         ("wqkv", pltpu.VMEM((1024, 3072), BF16)),

time: 124 us -> 112 us (0.903)
  Pallas kernels: 123 us -> 111 us
    pallas_call x1, Pallas kernels: 121 us -> 109 us  [relay(): pl.pallas_call(functools.partial(relay_kernel, names), out_shape=[jax.Sha...]
where the time goes in v3:
time: 112 us
  Pallas kernels  111 us (99%)
    pallas_call x1, Pallas kernels, relay(): pl.pallas_call(functools.partial(relay_kernel, names), out_shape=[jax.Sha...  109 us
    pallas_call x1, Pallas kernels, settle(): pl.pallas_call(functools.partial(settle_kernel, len(arrays)), out_shape=[...  2.24 us

profile of v3, /device:TPU:1, one launch (start us, length us, event | category | flops | bytes accessed | tf_op | source)
XLA Modules:
  0.0 111.9 jit_solution(617622475409635721)
XLA Ops:
  0.6 108.8 %relay.1 = (bf16[1,2,1,128,1024]{4,3,2,1,0:T(8,128)(2,1)}, bf16[1,2,1,128,1024]{4,3,2,1,0:T(8,128)(2,1)}, f32[1,32,3072]{2,1,0:T(8,128)}, f32[32,1024]{1,0:T(8,128)}) custom-call(bf16[2,1,128,1024]{3,2,1,0:T(8,128)(2,1)} %refs_0_.1, s32[2,1,128]{2,1,0:T(1,128)} %refs_1_.1, bf16[1,1024,3072]{2,1,0:T(8,128)(2,1)} %refs_2_.1, bf16[1,1024,1024]{2,1,0:T(8,128)(2,1)} %refs_3_.1, ...), custom_call_target="tpu_custom_call" | custom-call | tf_op jit(solution)/shard_map/relay/pallas_call | solution.py:530
  109.5 2.2 %settle.1 = (bf16[1,2,1,128,1024]{4,3,2,1,0:T(8,128)(2,1)}, bf16[1,2,1,128,1024]{4,3,2,1,0:T(8,128)(2,1)}, f32[1,32,3072]{2,1,0:T(8,128)}, f32[32,1024]{1,0:T(8,128)}) custom-call(bf16[1,2,1,128,1024]{4,3,2,1,0:T(8,128)(2,1)} %get-tuple-element.12.refs_0_, bf16[1,2,1,128,1024]{4,3,2,1,0:T(8,128)(2,1)} %get-tuple-element.13.refs_1_, ...), custom_call_target="tpu_custom_call" | custom-call | tf_op jit(solution)/shard_map/settle/pallas_call | solution.py:558

commit v4 on v3

--- a/solution.py
+++ b/solution.py
@@ -12,6 +12,8 @@
 F32 = jnp.float32
 EPSILON = 1e-6
 MESH = pl.DeviceIdType.MESH
+CHUNKS = (slice(0, 768), slice(768, 1024))
+HEAD, TAIL = CHUNKS
 
 
 def dg(a,b,ca=1,cb=0): return lax.dot_general(a,b,(((ca,),(cb,)),((),())),preferred_element_type=F32)
@@ -38,23 +40,37 @@
 
 def normalise(m, r):
     x = r.xin[m].astype(F32)
-    centred = x - jnp.mean(x, axis=-1, keepdims=True)
+    average = jnp.mean(x, axis=-1, keepdims=True)
+    centred = x - average
     inverse = lax.rsqrt(jnp.mean(centred * centred, axis=-1, keepdims=True) + EPSILON)
     r.xinv[m] = jnp.broadcast_to(inverse, (128, 128))
     r.normed[m] = (centred * inverse).astype(BF16)
-
-
-def attend(m, r):
+    return average, inverse
+
+
+def project_head(m, kind, r):
+    for j in range(6):
+        c = slice(512 * j, 512 * j + 512)
+        r.begun[:, c] = dg(r.acts[kind, m, :, HEAD], r.wqkv[HEAD, c])
+
+
+def attend(m, kind, r):
     queries_in = jnp.broadcast_to(r.segments[m].astype(F32), (128, 128))
     allowed = queries_in == queries_in.T
     allowed = jnp.concatenate([allowed, allowed], axis=1)
-    normed = r.normed[m]
+    rest = r.acts[kind, m, :, TAIL]
+    raw = 1.0 - kind.astype(F32)
+    average, inverse = normalise(m, r)
+    average = average * raw
+    inverse = inverse * raw + (1.0 - raw)
     live = {}
 
     def project(quad):
         for name, start in (("q", 0), ("k", 1024), ("v", 2048)):
             column = start + 256 * quad
-            live[name, quad] = dg(normed, r.wqkv[:, column : column + 256])
+            c = slice(column, column + 256)
+            product = r.begun[:, c] + dg(rest, r.wqkv[TAIL, c])
+            live[name, quad] = (product - average * r.columns[:1, c]) * inverse
 
     def norms(quad):
         for half in range(2):
@@ -93,19 +109,27 @@
             stage(quad)
 
 
-def project_out(m, r):
+def project_out(m, r, chunk):
     mixed = r.mixed[m]
-    for j in range(4):
-        c = slice(256*j, 256*j+256)
+    for start in range(chunk.start, chunk.stop, 256):
+        c = slice(start, start + 256)
         branch = dg(mixed, r.wout[:, c])
         r.xout[m, :, c] = (r.xin[m, :, c].astype(F32) + branch).astype(BF16)
 
+
+def mixed_pull_head(m, r):
+    for j in range(4):
+        c = slice(256 * j, 256 * j + 256)
+        r.gn[:, c] = dg(r.gin[m, :, HEAD], r.wout_t[HEAD, c])
+
+
 def attend_pull(m, r):
-    g = r.gin[m]
+    rest = r.gin[m, :, TAIL]
     live = {}
 
     def project(quad):
-        go4 = dg(g, r.wout_t[:, 256 * quad : 256 * quad + 256]).astype(BF16)
+        c = slice(256 * quad, 256 * quad + 256)
+        go4 = (r.gn[:, c] + dg(rest, r.wout_t[TAIL, c])).astype(BF16)
         for half in range(2):
             live["go", 2 * quad + half] = go4[:, 128 * half : 128 * half + 128].T
 
@@ -165,6 +189,9 @@
     for j in range(8):
         r.wqkv_t[:, 128*j:128*j+128] = r.wqkv[128*j:128*j+128, :].T
         r.wout_t[:, 128*j:128*j+128] = r.wout[128*j:128*j+128, :].T
+    for j in range(6):
+        c = slice(512 * j, 512 * j + 512)
+        r.columns[:, c] = dg(jnp.ones((16, 1024), BF16), r.wqkv[:, c])
 
 
 def spread(r, name, column, rows):
@@ -181,6 +208,7 @@
 
 def relay_kernel(names, *refs):
     r = types.SimpleNamespace(**dict(zip(names, refs)))
+    r.xin, r.normed = r.acts.at[0], r.acts.at[1]
     section = lax.axis_index("section")
     last = lax.axis_size("section") - 1
     after = lax.rem(section + 1, last + 1)
@@ -194,11 +222,13 @@
     partner = place + 1 - 2 * core
     y_peers = {a: place + 8 * (swap(y, a) - y) for a in (1, 3)}
     z_peers = {a: place + 2 * (swap(z, a) - z) for a in (1, 3)}
-    early = jnp.logical_or(jnp.logical_not(is_first), core == 1)
+    early = jnp.logical_not(is_first)
+    kind = (last - section) // last
 
     loads = [
-        pltpu.make_async_copy(r.w_qkv_hbm.at[0], r.wqkv, r.load.at[0]),
-        pltpu.make_async_copy(r.w_out_hbm.at[0], r.wout, r.load.at[1]),
+        pltpu.make_async_copy(r.w_qkv_hbm.at[0, pl.ds(0, 768)], r.wqkv.at[pl.ds(0, 768)], r.load.at[0]),
+        pltpu.make_async_copy(r.w_qkv_hbm.at[0, pl.ds(768, 256)], r.wqkv.at[pl.ds(768, 256)], r.load.at[1]),
+        pltpu.make_async_copy(r.w_out_hbm.at[0], r.wout, r.load.at[6]),
     ]
 
     def entry(m):
@@ -207,17 +237,19 @@
     def end_gradient(m):
         return pltpu.make_async_copy(r.cotangent.at[m, 0], r.gin.at[m], r.load.at[4 + m])
 
-    def pass_on(m):
+    def pass_on(m, i):
+        c = pl.ds(CHUNKS[i].start, CHUNKS[i].stop - CHUNKS[i].start)
         return pltpu.make_async_remote_copy(
-            src_ref=r.xout.at[m], dst_ref=r.xin.at[m],
-            send_sem=r.x_send.at[m], recv_sem=r.x_recv.at[m],
+            src_ref=r.xout.at[m, :, c], dst_ref=r.acts.at[0, m, :, c],
+            send_sem=r.x_send.at[m, i], recv_sem=r.x_recv.at[m, i],
             device_id={"section": after}, device_id_type=MESH,
         )
 
-    def pass_back(m):
+    def pass_back(m, i):
+        c = pl.ds(CHUNKS[i].start, CHUNKS[i].stop - CHUNKS[i].start)
         return pltpu.make_async_remote_copy(
-            src_ref=r.gout.at[m], dst_ref=r.gin.at[m],
-            send_sem=r.g_send.at[m], recv_sem=r.g_recv.at[m],
+            src_ref=r.gout.at[m, :, c], dst_ref=r.gin.at[m, :, c],
+            send_sem=r.g_send.at[m, i], recv_sem=r.g_recv.at[m, i],
             device_id={"section": before}, device_id_type=MESH,
         )
 
@@ -306,8 +338,7 @@
         for m in range(2):
             entry(m).start()
 
-    for load in loads:
-        load.start()
+    loads[0].start()
 
     @pl.when(is_last)
     def _():
@@ -322,6 +353,8 @@
 
     @pl.when(early)
     def _():
+        for load in loads[1:]:
+            load.start()
         for load in loads:
             load.wait()
         transpose_weights(r)
@@ -330,20 +363,34 @@
         @pl.when(is_first)
         def _():
             entry(m).wait()
+            normalise(m, r)
 
         @pl.when(jnp.logical_not(is_first))
         def _():
-            pass_on(m).wait_recv()
-
-        normalise(m, r)
-
-        @pl.when(jnp.logical_and(m == 0, jnp.logical_not(early)))
-        def _():
-            for load in loads:
+            pass_on(m, 0).wait_recv()
+
+        opening = jnp.logical_and(m == 0, jnp.logical_not(early))
+
+        @pl.when(opening)
+        def _():
+            loads[0].wait()
+            for load in loads[1:]:
+                load.start()
+
+        project_head(m, kind, r)
+
+        @pl.when(jnp.logical_not(is_first))
+        def _():
+            pass_on(m, 1).wait_recv()
+
+        @pl.when(opening)
+        def _():
+            r.columns[...] = jnp.zeros((16, 3072), F32)
+            for load in loads[1:]:
                 load.wait()
 
-        attend(m, r)
-        project_out(m, r)
+        attend(m, kind, r)
+        project_out(m, r, HEAD)
 
         @pl.when(m == 0)
         def _():
@@ -351,7 +398,13 @@
 
         @pl.when(jnp.logical_not(is_last))
         def _():
-            pass_on(m).start()
+            pass_on(m, 0).start()
+
+        project_out(m, r, TAIL)
+
+        @pl.when(jnp.logical_not(is_last))
+        def _():
+            pass_on(m, 1).start()
 
         keep_output(m).start()
         share("normed", m, 0).start()
@@ -380,7 +433,13 @@
 
         @pl.when(jnp.logical_not(is_last))
         def _():
-            pass_back(m).wait_recv()
+            pass_back(m, 0).wait_recv()
+
+        mixed_pull_head(m, r)
+
+        @pl.when(jnp.logical_not(is_last))
+        def _():
+            pass_back(m, 1).wait_recv()
 
         share("gin", m, 2).start()
         attend_pull(m, r)
@@ -389,7 +448,8 @@
         @pl.when(jnp.logical_not(is_first))
         def _():
             input_pull(m, r)
-            pass_back(m).start()
+            pass_back(m, 0).start()
+            pass_back(m, 1).start()
             keep_gradient(m).start()
 
     turns = section // last
@@ -463,11 +523,13 @@
 
         @pl.when(jnp.logical_not(is_last))
         def _():
-            pass_on(m).wait_send()
+            pass_on(m, 0).wait_send()
+            pass_on(m, 1).wait_send()
 
         @pl.when(jnp.logical_not(is_first))
         def _():
-            pass_back(m).wait_send()
+            pass_back(m, 0).wait_send()
+            pass_back(m, 1).wait_send()
 
 
 def relay(patches, segments, w_qkv, w_out, cotangent):
@@ -487,11 +549,12 @@
     ]
     block = (2, 128, 1024)
     scratch = [
-        ("xin", pltpu.VMEM(block, BF16)),
+        ("acts", pltpu.VMEM((2,) + block, BF16)),
+        ("begun", pltpu.VMEM((128, 3072), F32)),
+        ("columns", pltpu.VMEM((16, 3072), F32)),
         ("gin", pltpu.VMEM(block, BF16)),
         ("xout", pltpu.VMEM(block, BF16)),
         ("gout", pltpu.VMEM(block, BF16)),
-        ("normed", pltpu.VMEM(block, BF16)),
         ("mixed", pltpu.VMEM(block, BF16)),
         ("their_normed", pltpu.VMEM(block, BF16)),
         ("their_mixed", pltpu.VMEM(block, BF16)),
@@ -519,12 +582,12 @@
         ("qi", pltpu.VMEM((2, 8, 2, 128), F32)),
         ("ki", pltpu.VMEM((2, 8, 2, 128), F32)),
         ("probs", pltpu.VMEM((2, 8, 128, 256), BF16)),
-        ("load", pltpu.SemaphoreType.DMA((6,))),
+        ("load", pltpu.SemaphoreType.DMA((7,))),
         ("store", pltpu.SemaphoreType.DMA((4,))),
-        ("x_send", pltpu.SemaphoreType.DMA((2,))),
-        ("x_recv", pltpu.SemaphoreType.DMA((2,))),
-        ("g_send", pltpu.SemaphoreType.DMA((2,))),
-        ("g_recv", pltpu.SemaphoreType.DMA((2,))),
+        ("x_send", pltpu.SemaphoreType.DMA((2, 2))),
+        ("x_recv", pltpu.SemaphoreType.DMA((2, 2))),
+        ("g_send", pltpu.SemaphoreType.DMA((2, 2))),
+        ("g_recv", pltpu.SemaphoreType.DMA((2, 2))),
     ]
     names = [i[0] for i in inputs] + [o[0] for o in results] + [s[0] for s in scratch]
     return pl.pallas_call(

time: 112 us -> 104 us (0.929)
  Pallas kernels: 111 us -> 103 us
    pallas_call x1, Pallas kernels: 109 us -> 101 us  [relay(): pl.pallas_call(functools.partial(relay_kernel, names), out_shape=[jax.Sha...]
where the time goes in v4:
time: 104 us
  Pallas kernels  103 us (99%)
    pallas_call x1, Pallas kernels, relay(): pl.pallas_call(functools.partial(relay_kernel, names), out_shape=[jax.Sha...  101 us
    pallas_call x1, Pallas kernels, settle(): pl.pallas_call(functools.partial(settle_kernel, len(arrays)), out_shape=[...  2.24 us

profile of v4, /device:TPU:1, one launch (start us, length us, event | category | flops | bytes accessed | tf_op | source)
XLA Modules:
  0.0 104.3 jit_solution(4606884663306108779)
XLA Ops:
  0.6 101.3 %relay.1 = (bf16[1,2,1,128,1024]{4,3,2,1,0:T(8,128)(2,1)}, bf16[1,2,1,128,1024]{4,3,2,1,0:T(8,128)(2,1)}, f32[1,32,3072]{2,1,0:T(8,128)}, f32[32,1024]{1,0:T(8,128)}) custom-call(bf16[2,1,128,1024]{3,2,1,0:T(8,128)(2,1)} %refs_0_.1, s32[2,1,128]{2,1,0:T(1,128)} %refs_1_.1, bf16[1,1024,3072]{2,1,0:T(8,128)(2,1)} %refs_2_.1, bf16[1,1024,1024]{2,1,0:T(8,128)(2,1)} %refs_3_.1, ...), custom_call_target="tpu_custom_call" | custom-call | tf_op jit(solution)/shard_map/relay/pallas_call | solution.py:593
  101.9 2.2 %settle.1 = (bf16[1,2,1,128,1024]{4,3,2,1,0:T(8,128)(2,1)}, bf16[1,2,1,128,1024]{4,3,2,1,0:T(8,128)(2,1)}, f32[1,32,3072]{2,1,0:T(8,128)}, f32[32,1024]{1,0:T(8,128)}) custom-call(bf16[1,2,1,128,1024]{4,3,2,1,0:T(8,128)(2,1)} %get-tuple-element.12.refs_0_, bf16[1,2,1,128,1024]{4,3,2,1,0:T(8,128)(2,1)} %get-tuple-element.13.refs_1_, ...), custom_call_target="tpu_custom_call" | custom-call | tf_op jit(solution)/shard_map/settle/pallas_call | solution.py:621

commit v5 on v4

--- a/solution.py
+++ b/solution.py
@@ -23,6 +23,12 @@
     top = jnp.concatenate([pair[:64], blank], axis=1)
     bottom = jnp.concatenate([blank, pair[64:]], axis=1)
     return jnp.concatenate([top, bottom], axis=0)
+
+def block_diagonal_rows(pair):
+    left = lax.broadcasted_iota(jnp.int32, pair.shape, 1) < 64
+    blank = jnp.zeros_like(pair)
+    return jnp.concatenate([jnp.where(left, pair, blank), jnp.where(left, blank, pair)], axis=0)
+
 
 def head_norm(rows):
     grouped = rows.reshape(2, 64, rows.shape[1])
@@ -131,7 +137,8 @@
         c = slice(256 * quad, 256 * quad + 256)
         go4 = (r.gn[:, c] + dg(rest, r.wout_t[TAIL, c])).astype(BF16)
         for half in range(2):
-            live["go", 2 * quad + half] = go4[:, 128 * half : 128 * half + 128].T
+            go = go4[:, 128 * half : 128 * half + 128]
+            live["rows", 2 * quad + half], live["go", 2 * quad + half] = go, go.T
 
     def probs_pull(quad):
         for pair in (2 * quad, 2 * quad + 1):
@@ -139,9 +146,8 @@
 
     def values_pull(quad):
         for pair in (2 * quad, 2 * quad + 1):
-            go, p = live["go", pair], r.probs[m, pair]
-            gv = [dg(go[64 * i : 64 * i + 64], p[:, 128 * i : 128 * i + 128], 1, 1) for i in range(2)]
-            live["gv", pair] = jnp.concatenate(gv, axis=0).astype(BF16)
+            gv = dg(r.probs[m, pair], block_diagonal_rows(live["rows", pair]))
+            r.gproj[m, :, 2048 + 128 * pair : 2176 + 128 * pair] = gv.astype(BF16)
 
     def scores_pull(quad):
         for pair in (2 * quad, 2 * quad + 1):
@@ -154,7 +160,7 @@
             ds, kt, qs = live["ds", pair], r.kt[m, pair], r.qs[m, pair]
             cut = [(slice(64 * i, 64 * i + 64), slice(128 * i, 128 * i + 128)) for i in range(2)]
             live["gq", pair] = jnp.concatenate([dg(kt[i], ds[:, c]) for i, c in cut], axis=0)
-            live["gk", pair] = jnp.concatenate([dg(qs[i], ds[:, c], 1, 1) for i, c in cut], axis=0)
+            live["gk", pair] = dg(ds, block_diagonal_rows(qs.T)).T
 
     def norms_pull(quad):
         for pair in (2 * quad, 2 * quad + 1):
@@ -165,7 +171,7 @@
 
     def turn(quad):
         for pair in (2 * quad, 2 * quad + 1):
-            for name, start in (("gq", 0), ("gk", 1024), ("gv", 2048)):
+            for name, start in (("gq", 0), ("gk", 1024)):
                 column = start + 128 * pair
                 r.gproj[m, :, column : column + 128] = live[name, pair].T
 
@@ -220,8 +226,8 @@
     z = lax.rem(place // 2, 4)
     y = place // 8
     partner = place + 1 - 2 * core
-    y_peers = {a: place + 8 * (swap(y, a) - y) for a in (1, 3)}
-    z_peers = {a: place + 2 * (swap(z, a) - z) for a in (1, 3)}
+    y_peers = {a: place + 8 * (swap(y, a) - y) for a in (1, 2, 3)}
+    z_peers = {a: place + 2 * (swap(z, a) - z) for a in (1, 2, 3)}
     early = jnp.logical_not(is_first)
     kind = (last - section) // last
 
@@ -286,12 +292,9 @@
             source, target, peer = block(half, j, swap(p, a)), r.near_in, p_peers[a]
         elif step == 2:
             source, target, peer = r.far_sum.at[half, j], r.last_in, p_peers[b]
-        elif step == 3:
-            source, target, peer = r.row.at[half, j, swap(q, 2)], r.row_far_in, q_peers[a]
-        elif step == 4:
-            source, target, peer = r.row.at[half, j, swap(q, a)], r.row_near_in, q_peers[a]
         else:
-            source, target, peer = r.row_far_sum.at[half, j], r.row_last_in, q_peers[b]
+            a = step - 2
+            source, target, peer = r.row.at[half, j, swap(q, a)], r.row_in.at[a - 1], q_peers[a]
         return pltpu.make_async_remote_copy(
             src_ref=source, dst_ref=target.at[half, j],
             send_sem=r.sum_send.at[half, j, step], recv_sem=r.sum_recv.at[half, j, step],
@@ -311,22 +314,16 @@
         send(half, j, 2).wait_recv()
         total = block(half, j, p)[...].astype(F32) + r.near_in[half, j].astype(F32)
         r.row[half, j] = (total + r.last_in[half, j].astype(F32)).astype(BF16)
-        send(half, j, 3).start()
-        send(half, j, 4).start()
+        for step in (3, 4, 5):
+            send(half, j, step).start()
 
     def sum_three(half, j):
         _, (q, _) = axes(half)
-        send(half, j, 3).wait_recv()
-        held = r.row[half, j, swap(q, masks(j)[1])].astype(F32)
-        r.row_far_sum[half, j] = (held + r.row_far_in[half, j].astype(F32)).astype(BF16)
-        send(half, j, 5).start()
-
-    def sum_four(half, j):
-        _, (q, _) = axes(half)
-        send(half, j, 4).wait_recv()
-        send(half, j, 5).wait_recv()
-        total = r.row[half, j, q].astype(F32) + r.row_near_in[half, j].astype(F32)
-        total = total + r.row_last_in[half, j].astype(F32)
+        total = r.row[half, j, q].astype(F32)
+        for step in (3, 4, 5):
+            send(half, j, step).wait_recv()
+        for k in range(3):
+            total = total + r.row_in[k, half, j].astype(F32)
         column = 2048 * half + 512 * j
         if column < 3072:
             r.total_qkv[0, :, column : column + 512] = total
@@ -394,7 +391,7 @@
 
         @pl.when(m == 0)
         def _():
-            pl.semaphore_wait(barrier, 7)
+            pl.semaphore_wait(barrier, 9)
 
         @pl.when(jnp.logical_not(is_last))
         def _():
@@ -503,8 +500,8 @@
             input_pull(m, r)
             keep_gradient(m).start()
 
-    stages = (sum_one, sum_two, sum_three, sum_four)
-    lags = (0, 3, 6, 9)
+    stages = (sum_one, sum_two, sum_three)
+    lags = (0, 3, 6)
     for step in range(len(pieces) + lags[-1]):
         for lag, stage in zip(lags, stages):
             if 0 <= step - lag < len(pieces):
@@ -564,7 +561,7 @@
         ("gin_t", pltpu.VMEM((16, 2, 32, 512), BF16)),
         ("part", pltpu.VMEM((2, 4, 4, 4, 32, 512), BF16)),
         *((name, pltpu.VMEM((2, 4, 4, 32, 512), BF16)) for name in ("far_in", "near_in", "far_sum", "last_in", "row")),
-        *((name, pltpu.VMEM((2, 4, 32, 512), BF16)) for name in ("row_far_in", "row_near_in", "row_far_sum", "row_last_in")),
+        ("row_in", pltpu.VMEM((3, 2, 4, 32, 512), BF16)),
         ("sum_send", pltpu.SemaphoreType.DMA((2, 4, 6))),
         ("sum_recv", pltpu.SemaphoreType.DMA((2, 4, 6))),
         ("share_send", pltpu.SemaphoreType.DMA((4, 2))),

time: 104 us -> 104 us (level)
  no operation moved by 1% of the time
where the time goes in v5:
time: 104 us
  Pallas kernels  103 us (99%)
    pallas_call x1, Pallas kernels, relay(): pl.pallas_call(functools.partial(relay_kernel, names), out_shape=[jax.Sha...  101 us
    pallas_call x1, Pallas kernels, settle(): pl.pallas_call(functools.partial(settle_kernel, len(arrays)), out_shape=[...  2.24 us

profile of v5, /device:TPU:1, one launch (start us, length us, event | category | flops | bytes accessed | tf_op | source)
XLA Modules:
  0.0 103.6 jit_solution(12684890843447758017)
XLA Ops:
  0.6 100.6 %relay.1 = (bf16[1,2,1,128,1024]{4,3,2,1,0:T(8,128)(2,1)}, bf16[1,2,1,128,1024]{4,3,2,1,0:T(8,128)(2,1)}, f32[1,32,3072]{2,1,0:T(8,128)}, f32[32,1024]{1,0:T(8,128)}) custom-call(bf16[2,1,128,1024]{3,2,1,0:T(8,128)(2,1)} %refs_0_.1, s32[2,1,128]{2,1,0:T(1,128)} %refs_1_.1, bf16[1,1024,3072]{2,1,0:T(8,128)(2,1)} %refs_2_.1, bf16[1,1024,1024]{2,1,0:T(8,128)(2,1)} %refs_3_.1, ...), custom_call_target="tpu_custom_call" | custom-call | tf_op jit(solution)/shard_map/relay/pallas_call | solution.py:590
  101.2 2.2 %settle.1 = (bf16[1,2,1,128,1024]{4,3,2,1,0:T(8,128)(2,1)}, bf16[1,2,1,128,1024]{4,3,2,1,0:T(8,128)(2,1)}, f32[1,32,3072]{2,1,0:T(8,128)}, f32[32,1024]{1,0:T(8,128)}) custom-call(bf16[1,2,1,128,1024]{4,3,2,1,0:T(8,128)(2,1)} %get-tuple-element.12.refs_0_, bf16[1,2,1,128,1024]{4,3,2,1,0:T(8,128)(2,1)} %get-tuple-element.13.refs_1_, ...), custom_call_target="tpu_custom_call" | custom-call | tf_op jit(solution)/shard_map/settle/pallas_call | solution.py:618

commit v6 on v5

--- a/solution.py
+++ b/solution.py
@@ -237,6 +237,8 @@
         pltpu.make_async_copy(r.w_out_hbm.at[0], r.wout, r.load.at[6]),
     ]
 
+    labels = pltpu.make_async_copy(r.segments_hbm, r.segments, r.load.at[7])
+
     def entry(m):
         return pltpu.make_async_copy(r.patches.at[m, 0], r.xin.at[m], r.load.at[2 + m])
 
@@ -335,6 +337,7 @@
         for m in range(2):
             entry(m).start()
 
+    labels.start()
     loads[0].start()
 
     @pl.when(is_last)
@@ -385,6 +388,10 @@
             r.columns[...] = jnp.zeros((16, 3072), F32)
             for load in loads[1:]:
                 load.wait()
+
+        @pl.when(m == 0)
+        def _():
+            labels.wait()
 
         attend(m, kind, r)
         project_out(m, r, HEAD)
@@ -532,7 +539,7 @@
 def relay(patches, segments, w_qkv, w_out, cotangent):
     inputs = [
         ("patches", patches, pl.ANY),
-        ("segments", segments, pltpu.VMEM),
+        ("segments_hbm", segments, pltpu.HBM),
         ("w_qkv_hbm", w_qkv, pl.ANY),
         ("w_out_hbm", w_out, pl.ANY),
         ("cotangent", cotangent, pl.ANY),
@@ -547,6 +554,7 @@
     block = (2, 128, 1024)
     scratch = [
         ("acts", pltpu.VMEM((2,) + block, BF16)),
+        ("segments", pltpu.VMEM(segments.shape, jnp.int32)),
         ("begun", pltpu.VMEM((128, 3072), F32)),
         ("columns", pltpu.VMEM((16, 3072), F32)),
         ("gin", pltpu.VMEM(block, BF16)),
@@ -579,7 +587,7 @@
         ("qi", pltpu.VMEM((2, 8, 2, 128), F32)),
         ("ki", pltpu.VMEM((2, 8, 2, 128), F32)),
         ("probs", pltpu.VMEM((2, 8, 128, 256), BF16)),
-        ("load", pltpu.SemaphoreType.DMA((7,))),
+        ("load", pltpu.SemaphoreType.DMA((8,))),
         ("store", pltpu.SemaphoreType.DMA((4,))),
         ("x_send", pltpu.SemaphoreType.DMA((2, 2))),
         ("x_recv", pltpu.SemaphoreType.DMA((2, 2))),

time: 104 us -> 103 us (level)
  no operation moved by 1% of the time
where the time goes in v6:
time: 103 us
  Pallas kernels  102 us (99%)
    pallas_call x1, Pallas kernels, relay(): pl.pallas_call(functools.partial(relay_kernel, names), out_shape=[jax.Sha...  100 us
    pallas_call x1, Pallas kernels, settle(): pl.pallas_call(functools.partial(settle_kernel, len(arrays)), out_shape=[...  2.24 us

profile of v6, /device:TPU:1, one launch (start us, length us, event | category | flops | bytes accessed | tf_op | source)
XLA Modules:
  0.0 103.1 jit_solution(10756705592289056400)
XLA Ops:
  0.6 100.0 %relay.1 = (bf16[1,2,1,128,1024]{4,3,2,1,0:T(8,128)(2,1)}, bf16[1,2,1,128,1024]{4,3,2,1,0:T(8,128)(2,1)}, f32[1,32,3072]{2,1,0:T(8,128)}, f32[32,1024]{1,0:T(8,128)}) custom-call(bf16[2,1,128,1024]{3,2,1,0:T(8,128)(2,1)} %refs_0_.1, s32[2,1,128]{2,1,0:T(1,128)} %refs_1_.1, bf16[1,1024,3072]{2,1,0:T(8,128)(2,1)} %refs_2_.1, bf16[1,1024,1024]{2,1,0:T(8,128)(2,1)} %refs_3_.1, ...), custom_call_target="tpu_custom_call" | custom-call | tf_op jit(solution)/shard_map/relay/pallas_call | solution.py:598
  100.7 2.2 %settle.1 = (bf16[1,2,1,128,1024]{4,3,2,1,0:T(8,128)(2,1)}, bf16[1,2,1,128,1024]{4,3,2,1,0:T(8,128)(2,1)}, f32[1,32,3072]{2,1,0:T(8,128)}, f32[32,1024]{1,0:T(8,128)}) custom-call(bf16[1,2,1,128,1024]{4,3,2,1,0:T(8,128)(2,1)} %get-tuple-element.12.refs_0_, bf16[1,2,1,128,1024]{4,3,2,1,0:T(8,128)(2,1)} %get-tuple-element.13.refs_1_, ...), custom_call_target="tpu_custom_call" | custom-call | tf_op jit(solution)/shard_map/settle/pallas_call | solution.py:626
